TPU v7x, 256 devices: a whole 4x4x8 slice. The times are simulated.
256 devices in a mesh: arc: 16 (over x, y), ord: 16 (over z, core).
Axes of the slice: x: 4, y: 4, z: 8, core: 2. Of those that a mesh axis runs over, the one named last changes fastest.
Arguments:
- obs_colat: float32 [393216], P('arc'), may hold values from 0.12 to 3.0216
- obs_lon: float32 [393216], P('arc'), may hold values from -3.140625 to 3.140625
- obs_value: bfloat16 [393216], P('arc'), may hold values from -6 to 6
- obs_arc: int32 [393216], P('arc'), may hold values from 0 to 16, as said below
- reg_weight: float32 [32, 252], P('ord'), may hold values from 0.1 to 1
Outputs:
- solution: float32 [32, 252], P('ord')
- arc_bias: float32 [256], P('arc')
- residual: float32 [393216], P(('arc', 'ord'))
Inputs may be any that keep to these rules, and one draw needn't show every extreme that they name: `obs_arc`: within each arc device's 24576 slots the values never fall, each of 0 to 15 names at least one slot, and the value 16 marks unused slots, which come last. Every arc device uses at least 6144 slots, and some arc device uses all 24576.
All inputs are finite; a program needn't handle non-finite values.
Results may differ from a plain program's by a relative error of at most 0.0055.
Values sent between devices are 32-bit elements; how exact they have to be, the bound alone decides.
A program may use at most 320 MiB of HBM per device.

v0:
```python
import math

import jax
import jax.numpy as jnp
import numpy as np
from jax import lax
from jax.sharding import PartitionSpec as P

DEG = 250
ARC_DEV = 16


def log_sectoral():
    increments = [0.0, 0.5 * math.log(3.0)] + [
        0.5 * math.log((2.0 * degree_now + 1.0) / (2.0 * degree_now))
        for degree_now in range(2, DEG + 1)
    ]
    return jnp.asarray(np.cumsum(np.array(increments[: DEG + 1])), dtype=jnp.float32)


def design_columns(colatitude, longitude, arc_ids, first_order):
    pair_count = first_order.shape[0]
    observed = (arc_ids < ARC_DEV).astype(jnp.float32)
    orders = jnp.concatenate([first_order, DEG - first_order])
    offsets = jnp.concatenate([first_order, jnp.full((pair_count,), -1, jnp.int32)])
    order_float = orders.astype(jnp.float32)
    log_table = log_sectoral()
    log_coeff = jnp.sum(
        jnp.where(
            jnp.arange(DEG + 1, dtype=jnp.int32)[None, :] == orders[:, None],
            log_table[None, :],
            0.0,
        ),
        axis=1,
    )
    cosine = jnp.cos(colatitude)
    sine_theta = jnp.sin(colatitude)
    sectoral = jnp.exp(order_float[:, None] * jnp.log(sine_theta)[None, :] + log_coeff[:, None])
    phases = jnp.cos(order_float[:, None] * longitude[None, :]) * observed[None, :]

    def recurse(carried, column):
        previous, before = carried
        degree = column + offsets
        degree_float = degree.astype(jnp.float32)
        beyond_order = degree > orders
        denominator = jnp.maximum((degree_float - order_float) * (degree_float + order_float), 1.0)
        rising = jnp.where(
            beyond_order,
            jnp.sqrt(
                jnp.maximum((2.0 * degree_float - 1.0) * (2.0 * degree_float + 1.0), 0.0)
                / denominator
            ),
            0.0,
        )
        falling_top = jnp.maximum(
            (2.0 * degree_float + 1.0)
            * (degree_float + order_float - 1.0)
            * (degree_float - order_float - 1.0),
            0.0,
        )
        falling = jnp.where(
            beyond_order,
            jnp.sqrt(falling_top / (denominator * jnp.maximum(2.0 * degree_float - 3.0, 1.0))),
            0.0,
        )
        current = rising[:, None] * cosine[None, :] * previous - falling[:, None] * before
        current = jnp.where((degree == orders)[:, None], sectoral, current)
        emitted = jnp.where((degree <= DEG)[:, None], current, 0.0) * phases
        return (
            (current, previous),
            (emitted[:pair_count] + emitted[pair_count:]).astype(jnp.bfloat16),
        )

    initial = jnp.zeros((2 * pair_count, colatitude.shape[0]), jnp.float32)
    _, columns = lax.scan(
        recurse, (initial, initial), jnp.arange(DEG + 2, dtype=jnp.int32), unroll=12
    )
    return columns


def local_normals(columns, values, arc_ids):
    arc_member = jnp.arange(ARC_DEV, dtype=jnp.int32)[:, None] == arc_ids[None, :]
    counts = jnp.sum(arc_member.astype(jnp.float32), axis=1)
    member_half = arc_member.astype(jnp.bfloat16)
    weighted = jnp.where(arc_ids < ARC_DEV, values, jnp.zeros_like(values))
    normal_part = lax.dot_general(
        columns, columns, (((2,), (2,)), ((1,), (1,))), preferred_element_type=jnp.float32
    )
    arc_sums = jnp.einsum("cpr,kr->pkc", columns, member_half, preferred_element_type=jnp.float32)
    projected = jnp.einsum("cpr,r->pc", columns, weighted, preferred_element_type=jnp.float32)
    arc_target = jnp.einsum("kr,r->k", member_half, weighted, preferred_element_type=jnp.float32)
    scaled = arc_sums / counts[None, :, None]
    normal_part = normal_part - jnp.einsum(
        "pkc,pkd->pcd", scaled, arc_sums, precision=lax.Precision.HIGHEST
    )
    right_part = projected - jnp.einsum(
        "pkc,k->pc", arc_sums, arc_target / counts, precision=lax.Precision.HIGHEST
    )
    return (normal_part, right_part, arc_sums, arc_target, counts)


def solve_pairs(normal_sum, right_sum, regular, first_order, total_rows):
    block_width = normal_sum.shape[-1]
    column_ids = jnp.arange(block_width, dtype=jnp.int32)
    low_order = column_ids[None, :] < (DEG + 1 - first_order)[:, None]
    same_order = (low_order[:, :, None] == low_order[:, None, :]).astype(jnp.float32)
    matrix = (
        same_order * normal_sum / total_rows
        + jnp.eye(block_width, dtype=jnp.float32)[None, :, :] * regular[:, None, :]
    )
    factor = jnp.linalg.cholesky(matrix)
    target = (right_sum / math.sqrt(total_rows))[:, :, None]
    middle = lax.linalg.triangular_solve(factor, target, left_side=True, lower=True)
    solution = lax.linalg.triangular_solve(
        factor, middle, left_side=True, lower=True, transpose_a=True
    )
    return solution[:, :, 0]


def fit_rows(columns, solution):
    fitted = jnp.zeros((columns.shape[2],), jnp.float32)
    for pair_index in range(columns.shape[1]):
        fitted = fitted + jnp.dot(
            solution[pair_index],
            columns[:, pair_index, :].astype(jnp.float32),
            precision=lax.Precision.HIGHEST,
        )
    return fitted


def per_device(obs_colat, obs_lon, obs_value, obs_arc, reg_weight):
    pair_count = reg_weight.shape[0]
    rows_here = obs_colat.shape[0]
    arc_devices = lax.axis_size("arc")
    order_devices = lax.axis_size("ord")
    total_rows = rows_here * arc_devices
    root_total = math.sqrt(total_rows)
    first_order = lax.axis_index("ord") * pair_count + jnp.arange(pair_count, dtype=jnp.int32)
    columns = design_columns(obs_colat, obs_lon, obs_arc, first_order)
    normal_part, right_part, arc_sums, arc_target, counts = local_normals(
        columns, obs_value, obs_arc
    )
    normal_sum, right_sum = lax.psum((normal_part, right_part), "arc")
    solution = solve_pairs(normal_sum, right_sum, reg_weight, first_order, total_rows)
    share = rows_here // order_devices
    my_start = lax.axis_index("ord") * share
    partial_fit = fit_rows(columns, solution)
    fitted = lax.psum(partial_fit, "ord") / root_total
    arc_member = (jnp.arange(ARC_DEV, dtype=jnp.int32)[:, None] == obs_arc[None, :]).astype(
        jnp.float32
    )
    arc_bias = (arc_target - jnp.dot(arc_member, fitted, precision=lax.Precision.HIGHEST)) / counts
    bias_rows = jnp.sum(arc_member * arc_bias[:, None], axis=0)
    residual_all = jnp.where(
        obs_arc < ARC_DEV, obs_value.astype(jnp.float32) - fitted - bias_rows, 0.0
    )
    residual = lax.dynamic_slice_in_dim(residual_all, my_start, share)
    return (solution, arc_bias, residual)


def solution(mesh):
    placed = (P("arc"), P("arc"), P("arc"), P("arc"), P("ord", None))
    return jax.shard_map(
        per_device,
        mesh=mesh,
        in_specs=placed,
        out_specs=(P("ord", None), P("arc"), P(("arc", "ord"))),
        check_vma=False,
    )
```

profile of v0, /device:TPU:1, one launch (start us, length us, event | category | flops | bytes accessed | tf_op | source)
XLA Modules:
  0.0 1009.3 jit_solution(18286130901821636535)
XLA Ops:
  10.4 500.3 %while.22 = (s32[]{:T(128)}, f32[4,24576]{1,0:T(4,128)S(1)}, f32[4,24576]{1,0:T(4,128)S(1)}, bf16[21,12,2,24576]{3,2,1,0:T(2,128)(2,1)}, s32[21,12]{0,1:T(8,128)...) while((s32[]{:T(128)}, f32[4,24576]{1,0:T(4,128)S(1)}, ...), condition=%wide.region_2.3_spmd.clone.clone.clone, body=%wide.region_1.2_spmd.clone.clone.clone.sunk | while | flops 10421485 | bytes 23988944 | solution.py:75
  11.1 7.5 broadcast_compare_fusion.15
  18.8 5.6 fusion.131
  35.0 7.5 broadcast_compare_fusion.15
  42.7 5.6 fusion.131
  48.3 3.2 fusion.133
  58.8 7.5 broadcast_compare_fusion.15
  66.5 5.6 fusion.131
  72.1 3.2 fusion.133
  82.6 7.5 broadcast_compare_fusion.15
  90.3 5.6 fusion.131
  95.9 3.2 fusion.133
  106.4 7.5 broadcast_compare_fusion.15
  114.1 5.6 fusion.131
  119.7 3.2 fusion.133
  130.2 7.5 broadcast_compare_fusion.15
  137.9 5.6 fusion.131
  143.5 3.2 fusion.133
  154.0 7.5 broadcast_compare_fusion.15
  161.7 5.6 fusion.131
  167.3 3.2 fusion.133
  177.8 7.5 broadcast_compare_fusion.15
  185.5 5.6 fusion.131
  201.7 7.5 broadcast_compare_fusion.15
  209.4 5.6 fusion.131
  215.0 3.2 fusion.133
  225.5 7.5 broadcast_compare_fusion.15
  233.2 5.6 fusion.131
  238.8 3.2 fusion.133
  249.4 7.5 broadcast_compare_fusion.15
  257.1 5.6 fusion.131
  273.1 7.5 broadcast_compare_fusion.15
  280.8 5.6 fusion.131
  286.4 3.2 fusion.133
  297.0 7.5 broadcast_compare_fusion.15
  304.7 5.6 fusion.131
  320.8 7.5 broadcast_compare_fusion.15
  328.5 5.6 fusion.131
  344.7 7.5 broadcast_compare_fusion.15
  352.4 5.6 fusion.131
  368.5 7.5 broadcast_compare_fusion.15
  376.2 5.6 fusion.131
  392.3 7.5 broadcast_compare_fusion.15
  400.0 5.6 fusion.131
  416.2 7.5 broadcast_compare_fusion.15
  423.8 5.6 fusion.131
  440.0 7.5 broadcast_compare_fusion.15
  447.6 5.6 fusion.131
  463.8 7.5 broadcast_compare_fusion.15
  471.5 5.6 fusion.131
  487.6 7.5 broadcast_compare_fusion.15
  495.3 5.6 fusion.131
  510.7 24.1 %fusion.57 = f32[2,16,252]{2,1,0:T(8,128)S(1)} fusion(bf16[252,2,24576]{2,1,0:T(2,128)(2,1)} %bitcast.205, s32[24576]{0:T(1024)S(1)} %copy-done.2), kind=kOutput, calls=%fused_computation.208 | convolution fusion | flops 396754944 | bytes 24903168 | tf_op jit(solution)/shard_map/cpr,kr->pkc/dot_general | solution.py:89
  534.9 45.3 %fusion.45 = f32[2,252,252]{2,1,0:T(8,128)S(1)} fusion(bf16[252,2,24576]{2,1,0:T(2,128)(2,1)} %bitcast.206), kind=kOutput, calls=%fused_computation.192 | convolution fusion | flops 6242697216 | bytes 25280640 | tf_op jit(solution)/shard_map/dot_general | solution.py:86
  582.3 46.5 %fusion.114 = (bf16[252,1,24576]{2,1,0:T(2,128)(2,1)}, bf16[252,1,24576]{2,1,0:T(2,128)(2,1)}) fusion(bf16[252,2,24576]{2,1,0:T(2,128)(2,1)} %bitcast.207), kind=kLoop, calls=%fused_computation.293 | loop fusion | bytes 49545216 | tf_op jit(solution)/shard_map/slice | solution.py:125
  629.6 24.0 %fusion.43 = f32[1,252,2]{1,0,2:T(1,128)S(1)} fusion(bf16[24576,1,1]{0,1,2:T(2,128)(2,1)S(1)} %reshape.870, bf16[252,2,24576]{2,1,0:T(2,128)(2,1)} %bitcast.208), kind=kOutput, calls=%fused_computation.190 | convolution fusion | flops 24772608 | bytes 24823776 | tf_op jit(solution)/shard_map/cpr,r->pc/dot_general | solution.py:90
  653.7 62.6 %psum.22 = f32[2,252]{0,1:T(8,128)S(1)} all-reduce(f32[2,252]{0,1:T(8,128)S(1)} %bitcast_subtract_fusion), channel_id=1, replica_groups=mesh['arc'=16,'ord'=16] {'arc'}, use_global_device_ids=true, to_apply=%region_9.10 | all-reduce | flops 504 | bytes 4032 | tf_op jit(solution)/shard_map/psum | solution.py:143
  718.3 23.5 %custom-call.18 = f32[2,128,128]{2,1,0:T(8,128)S(1)} custom-call(f32[2,128,128]{2,1,0:T(8,128)S(1)} %cholesky.126), custom_call_target="Cholesky" | custom-call | tf_op jit(solution)/shard_map/jit(cholesky)/cholesky | solution.py:111
  741.8 19.7 %custom-call.19 = f32[2,1,128,128]{2,3,1,0:T(8,128)S(1)} custom-call(f32[2,1,128,128]{3,2,1,0:T(8,128)S(1)} %get-tuple-element.534), custom_call_target="InvertDiagBlocksLowerTriangular" | custom-call | tf_op jit(solution)/shard_map/jit(cholesky)/cholesky | solution.py:111
  762.2 22.7 %custom-call.20 = f32[2,124,124]{2,1,0:T(8,128)S(1)} custom-call(f32[2,124,124]{2,1,0:T(8,128)S(1)} %convolution_subtract_fusion.1), custom_call_target="Cholesky" | custom-call | tf_op jit(solution)/shard_map/jit(cholesky)/cholesky | solution.py:111
  785.5 39.3 %custom-call.21 = f32[2,2,128,128]{2,3,1,0:T(8,128)S(1)} custom-call(f32[2,2,128,128]{3,2,1,0:T(8,128)S(1)} %pad_maximum_fusion), custom_call_target="InvertDiagBlocksLowerTriangular" | custom-call | tf_op jit(solution)/shard_map/triangular_solve | solution.py:114
  826.8 27.4 %fusion.47 = f32[1,24576]{1,0:T(1,128)S(1)} fusion(bf16[252,1,24576]{2,1,0:T(2,128)(2,1)} %get-tuple-element.529, f32[2,128,1]{1,0,2:T(2,128)S(1)} %bitcast.215, f32[2,124,1]{1,0,2:T(2,128)S(1)} %bitcast.212), kind=kOutput, calls=%fused_computation.194 | convolution fusion | flops 74318080 | bytes 12486624 | tf_op jit(solution)/shard_map/dot_general | solution.py:123
  854.1 27.4 %fusion.50 = f32[1,24576]{1,0:T(1,128)S(1)} fusion(bf16[252,1,24576]{2,1,0:T(2,128)(2,1)} %get-tuple-element.530, f32[2,128,1]{1,0,2:T(2,128)S(1)} %bitcast.216, f32[2,124,1]{1,0,2:T(2,128)S(1)} %bitcast.213), kind=kOutput, calls=%fused_computation.197 | convolution fusion | flops 74318080 | bytes 12486624 | tf_op jit(solution)/shard_map/dot_general | solution.py:123
  882.8 116.3 %all-reduce.9.cloned.1.call-done = f32[24576]{0:T(1024)} async-done(((f32[24576]{0:T(1024)}), f32[24576]{0:T(1024)}) %all-reduce.9.cloned.1.call-update) | async-done | bytes 98320 | tf_op jit(solution)/shard_map/psum | solution.py:148
  (490 shorter events, 209.8 us)
Async XLA Ops:
  7.2 709.4 %all-reduce.7.cloned.1.call-start = ((), (), s32[]{:S(2)}) async-start(), calls=%async_computation | async-start | bytes 1048576 | tf_op jit(solution)/shard_map/psum | solution.py:143
  10.4 500.4 %copy-start.2 = (s32[24576]{0:T(1024)S(1)}, s32[24576]{0:T(1024)}, u32[]{:S(2)}) copy-start(s32[24576]{0:T(1024)} %param.11) | copy-start | bytes 294916
  18.8 5.6 copy-start
  42.6 5.6 copy-start
  66.5 5.6 copy-start
  90.3 5.6 copy-start
  114.1 5.6 copy-start
  137.9 5.6 copy-start
  161.7 5.6 copy-start
  185.5 5.6 copy-start
  209.4 5.6 copy-start
  233.2 5.6 copy-start
  257.0 5.6 copy-start
  280.8 5.6 copy-start
  304.7 5.6 copy-start
  328.5 5.6 copy-start
  352.4 5.6 copy-start
  376.2 5.6 copy-start
  400.0 5.6 copy-start
  423.8 5.6 copy-start
  447.6 5.6 copy-start
  471.5 5.6 copy-start
  495.3 5.6 copy-start
  580.2 2.0 copy-start.3
  582.0 417.1 %all-reduce.9.cloned.1.call-start = ((), (), s32[]{:S(2)}) async-start(), calls=%async_computation.1 | async-start | bytes 196608 | tf_op jit(solution)/shard_map/psum | solution.py:148
  653.6 63.1 %copy-start.4 = (f32[2,252]{1,0:T(2,128)S(1)}, f32[2,252]{1,0:T(2,128)}, u32[]{:S(2)}) copy-start(f32[2,252]{1,0:T(2,128)} %param.12) | copy-start | bytes 6052
  716.6 1.5 copy-start.1
  1001.1 1.1 copy-start.5
Sparse Core Ops, SparseCore 0:
  582.1 97.9 all-reduce.6
  882.4 116.7 all-reduce.8
where the time goes:
time: 1020 us; the launch traced here: 1010 us
  other arithmetic  554 us (54%)
  matrix products  154 us (15%)
  waiting for transfers between devices  116 us (11%)
  local copies, waits for them, and re-layouts  106 us (10%)
  blocking collectives  62.6 us (6%)
  between operations  14.6 us (1%)
    mul x63, other arithmetic, recurse(): emitted = jnp.where((degree <= DEG)[:, None], current, 0.0) * phases  246 us
    le x21, other arithmetic, recurse(): emitted = jnp.where((degree <= DEG)[:, None], current, 0.0) * phases  158 us
    psum x1, waiting for transfers between devices, per_device(): fitted = lax.psum(partial_fit, 'ord') / root_total  116 us
    another operation x10, other arithmetic, solve_pairs(): factor = jnp.linalg.cholesky(matrix)  66.2 us
    psum x1, blocking collectives, per_device(): normal_sum, right_sum = lax.psum((normal_part, right_part), 'arc')  62.6 us
    dot_general x2, matrix products, fit_rows(): jnp.dot(solution[pair_index], columns[:, pair_index, :].astype(jnp.float3...  54.8 us
    slice x1, local copies, waits for them, and re-layouts, fit_rows(): columns[:, pair_index, :].astype(jnp.float32)  46.5 us
    dot_general x1, matrix products, local_normals(): lax.dot_general(columns, columns, (((2,), (2,)), ((1,), (1,))), preferred...  45.3 us
  transfers between devices with their start and end apart: 2, of which 1 were waited for; matrix products, arithmetic and copies ran while one was open for 7% of the time, Pallas kernels for 0%

commit v1 on v0

v1 whole, which is shorter than its diff:
```python
import functools
import math

import jax
import jax.numpy as jnp
import numpy as np
from jax import lax
from jax.experimental import pallas as pl
from jax.experimental.pallas import tpu as pltpu
from jax.sharding import PartitionSpec as P

DEG = 250
BLOCK = 252
ARC_DEV = 16
WIDE = 256
ROWS = WIDE + ARC_DEV
VALUE_ROW = 255
CHUNK = 4096
TILES = CHUNK // 128
GROUPS = CHUNK // 1024
PANEL = 64
MESH = pl.DeviceIdType.MESH
MIB = 1024 * 1024
HIGHEST = lax.Precision.HIGHEST


def log_sectoral():
    increments = [0.0, 0.5 * math.log(3.0)] + [
        0.5 * math.log((2.0 * degree_now + 1.0) / (2.0 * degree_now))
        for degree_now in range(2, DEG + 1)
    ]
    return np.cumsum(np.array(increments[: DEG + 1])).astype(np.float32)


def recursion_table(pairs):
    table = np.zeros((pairs, 2, WIDE), np.float64)
    for pair in range(pairs):
        for column in range(BLOCK):
            low = column < DEG + 1 - pair
            order = pair if low else DEG - pair
            degree = pair + column if low else column - 1
            if degree == order:
                table[pair, 0, column] = 0.0
                table[pair, 1, column] = -1.0
                continue
            denominator = float((degree - order) * (degree + order))
            table[pair, 0, column] = math.sqrt(
                (2.0 * degree - 1.0) * (2.0 * degree + 1.0) / denominator
            )
            table[pair, 1, column] = math.sqrt(
                max((2.0 * degree + 1.0) * (degree + order - 1.0) * (degree - order - 1.0), 0.0)
                / (denominator * max(2.0 * degree - 3.0, 1.0))
            )
    return table.astype(np.float32)


def design_kernel(
    coef_ref,
    t_ref,
    seed_ref,
    value_ref,
    member_ref,
    counts_ref,
    design_ref,
    normal_ref,
    sums_ref,
    flat,
    total,
):
    step = pl.program_id(0)
    first_pair = lax.axis_index("ord") * 2
    starts = [DEG + 1 - first_pair, DEG - first_pair]
    chains = [(p, v) for p in range(2) for v in range(GROUPS)]

    @pl.when(step == 0)
    def _():
        total[...] = jnp.zeros_like(total)
        for tile in range(2 * TILES):
            flat[tile * WIDE + BLOCK - 4 : tile * WIDE + WIDE, :] = jnp.zeros(
                (WIDE - BLOCK + 4, 128), jnp.float32
            )

    t = [t_ref[v * 8 : v * 8 + 8, :] for v in range(GROUPS)]
    seed_low = tuple(seed_ref[p, v * 8 : v * 8 + 8, :] for p, v in chains)

    def place(p, v, column, data):
        flat[pl.ds((p * TILES + v * 8) * WIDE + column, 8, stride=WIDE), :] = data

    for p in range(2):
        for v in range(GROUPS):
            place(p, v, VALUE_ROW, value_ref[v * 8 : v * 8 + 8, :])

    def columns4(block, previous, before, seeds):
        for inner in range(4):
            column = block * 4 + inner
            rising = [coef_ref[p * 2 * WIDE + column] for p in range(2)]
            falling = [coef_ref[p * 2 * WIDE + WIDE + column] for p in range(2)]
            current = []
            for i, (p, v) in enumerate(chains):
                older = before[i]
                if seeds is not None:
                    older = jnp.where(column == starts[p], seeds[i], older)
                now = rising[p] * (t[v] * previous[i]) - falling[p] * older
                place(p, v, column, now)
                current.append(now)
            before, previous = previous, tuple(current)
        return previous, before

    zeros = tuple(jnp.zeros((8, 128), jnp.float32) for _ in chains)
    turn = starts[0] // 4
    carried = lax.fori_loop(
        0, turn, lambda block, c: columns4(block, c[0], c[1], None), (zeros, seed_low)
    )
    seed_high = tuple(seed_ref[2 + p, v * 8 : v * 8 + 8, :] for p, v in chains)
    carried = columns4(turn, carried[0], carried[1], seed_high)
    lax.fori_loop(
        turn + 1, BLOCK // 4, lambda block, c: columns4(block, c[0], c[1], None), carried
    )

    for p in range(2):
        design_ref[p, WIDE:ROWS, :] = member_ref[...]

        def convert(tile, _, p=p):
            lane = pl.multiple_of(tile * 128, 128)
            source = pl.multiple_of((p * TILES + tile) * WIDE, WIDE)
            design_ref[p, 0:WIDE, pl.ds(lane, 128)] = flat[pl.ds(source, WIDE), :].astype(
                jnp.bfloat16
            )
            return 0

        lax.fori_loop(0, TILES, convert, 0)

        def product(part, _, p=p):
            lane = pl.multiple_of(part * 1024, 1024)
            total[p] += lax.dot_general(
                design_ref[p, :, pl.ds(lane, 1024)],
                design_ref[p, 0:WIDE, pl.ds(lane, 1024)],
                (((1,), (1,)), ((), ())),
                preferred_element_type=jnp.float32,
            )
            return 0

        lax.fori_loop(0, CHUNK // 1024, product, 0)

    @pl.when(step == pl.num_programs(0) - 1)
    def _():
        for p in range(2):
            sums = total[p, WIDE:ROWS, :]
            counts = jnp.concatenate([counts_ref[...], counts_ref[...]], axis=1)
            scaled = sums / counts
            normal_ref[p] = total[p, 0:WIDE, :] - lax.dot_general(
                scaled,
                sums,
                (((0,), (0,)), ((), ())),
                precision=HIGHEST,
                preferred_element_type=jnp.float32,
            )
            sums_ref[p] = sums


def reduce_kernel(n, part_ref, out_ref, landed, send1, recv1, send2, recv2):
    me = lax.axis_index("arc")
    barrier = pltpu.get_barrier_semaphore()

    def greet(k, _):
        pl.semaphore_signal(
            barrier, inc=1, device_id={"arc": lax.rem(me + k, n)}, device_id_type=MESH
        )
        return 0

    lax.fori_loop(1, n, greet, 0)
    pl.semaphore_wait(barrier, n - 1)

    def scatter(k):
        peer = lax.rem(me + k, n)
        return pltpu.make_async_remote_copy(
            src_ref=part_ref.at[peer],
            dst_ref=landed.at[k],
            send_sem=send1.at[k],
            recv_sem=recv1.at[k],
            device_id={"arc": peer},
            device_id_type=MESH,
        )

    def gather(k):
        peer = lax.rem(me + k, n)
        return pltpu.make_async_remote_copy(
            src_ref=out_ref.at[me],
            dst_ref=out_ref.at[me],
            send_sem=send2.at[k],
            recv_sem=recv2.at[k],
            device_id={"arc": peer},
            device_id_type=MESH,
        )

    def start(make):
        def body(k, _):
            make(k).start()
            return 0

        lax.fori_loop(1, n, body, 0)

    def finish(make):
        def body(k, _):
            make(k).wait_send()
            return 0

        lax.fori_loop(1, n, body, 0)

    start(scatter)
    out_ref[me] = part_ref[me]

    def add(k, _):
        scatter(k).wait_recv()
        out_ref[me] = out_ref[me] + landed[k]
        return 0

    lax.fori_loop(1, n, add, 0)
    start(gather)

    def arrive(k, _):
        source = lax.rem(me - k + n, n)
        pltpu.make_async_remote_copy(
            src_ref=out_ref.at[source],
            dst_ref=out_ref.at[source],
            send_sem=send2.at[k],
            recv_sem=recv2.at[k],
            device_id={"arc": source},
            device_id_type=MESH,
        ).wait_recv()
        return 0

    lax.fori_loop(1, n, arrive, 0)
    finish(scatter)
    finish(gather)


def solve_kernel(
    total_rows,
    normal_ref,
    regular_ref,
    sums_ref,
    design_hbm,
    solution_ref,
    share_ref,
    design,
    work,
    copied,
    *,
    parts,
):
    first_pair = lax.axis_index("ord") * 2
    rows_here = design_hbm.shape[2]
    width = rows_here // parts
    copies = []
    for part in range(parts):
        span = pl.ds(part * width, width)
        copy = pltpu.make_async_copy(
            design_hbm.at[:, pl.ds(0, WIDE), span], design.at[:, :, span], copied.at[part]
        )
        copy.start()
        copies.append(copy)

    row_ids = lax.broadcasted_iota(jnp.int32, (WIDE, WIDE), 0)
    column_ids = lax.broadcasted_iota(jnp.int32, (WIDE, WIDE), 1)
    eye = row_ids == column_ids
    for p in range(2):
        border = DEG + 1 - first_pair - p
        real = (row_ids < BLOCK) & (column_ids < BLOCK)
        same = ((row_ids < border) == (column_ids < border)) & real
        normal = normal_ref[p]
        matrix = jnp.where(same, normal / total_rows, 0.0)
        matrix = matrix + jnp.where(eye, regular_ref[p], 0.0)
        right = jnp.where(row_ids < BLOCK, normal / math.sqrt(total_rows), 0.0)
        work[p] = jnp.where(column_ids == VALUE_ROW, right, matrix)

    for panel in range(WIDE // PANEL):
        top = panel * PANEL
        left = top // 128 * 128
        blocks = [work[p, top : top + PANEL, left:WIDE] for p in range(2)]
        panel_rows = lax.broadcasted_iota(jnp.int32, (PANEL, WIDE - left), 0)
        for k in range(min(PANEL, VALUE_ROW - top)):
            lane = top - left + k
            for p in range(2):
                block = blocks[p]
                row = block[k : k + 1, :]
                inverse = 1.0 / block[k : k + 1, lane : lane + 1]
                scaled = row * inverse
                updated = block - block[:, lane : lane + 1] * scaled
                blocks[p] = jnp.where(panel_rows == k, scaled, updated)
        for p in range(2):
            inner = top % 128
            weights = blocks[p]
            pieces = []
            if inner > 0:
                pieces.append(jnp.zeros((inner, WIDE - left), jnp.float32))
            pieces.append(weights)
            if inner + PANEL < 128:
                pieces.append(jnp.zeros((128 - inner - PANEL, WIDE - left), jnp.float32))
            tall = jnp.concatenate(pieces, axis=0) if len(pieces) > 1 else weights
            factor = work[p, :, left : left + 128]
            if panel == WIDE // PANEL - 1:
                lanes = lax.broadcasted_iota(jnp.int32, (WIDE, 128), 1)
                factor = jnp.where(lanes == VALUE_ROW - left, 0.0, factor)
            work[p, :, left:WIDE] = work[p, :, left:WIDE] - jnp.dot(
                factor, tall, precision=HIGHEST, preferred_element_type=jnp.float32
            )
            work[p, top : top + PANEL, left:WIDE] = weights

    solved = []
    for p in range(2):
        answer = jnp.where(eye, work[p, :, VALUE_ROW : VALUE_ROW + 1], 0.0)
        answer = jnp.sum(answer, axis=0, keepdims=True)
        lanes = lax.broadcasted_iota(jnp.int32, (1, WIDE), 1)
        answer = jnp.where(lanes < BLOCK, answer, 0.0)
        solved.append(answer)
        solution_ref[p : p + 1, :] = answer

    offsets = jnp.zeros((ARC_DEV, 1), jnp.float32)
    for p in range(2):
        offsets = offsets + jnp.sum(sums_ref[p] * solved[p], axis=1, keepdims=True)
    corner = lax.broadcasted_iota(jnp.int32, (ARC_DEV, 128), 0) == lax.broadcasted_iota(
        jnp.int32, (ARC_DEV, 128), 1
    )
    offset_row = jnp.sum(jnp.where(corner, offsets, 0.0), axis=0, keepdims=True)

    ranks = share_ref.shape[0]
    lines = rows_here // ranks // 128
    share_ref[...] = jnp.zeros_like(share_ref)
    for rank in range(ranks):
        share_ref[rank, lines : lines + 1, :] = offset_row

    split_rows = lax.broadcasted_iota(jnp.int32, (16, WIDE), 0)
    split = []
    for p in range(2):
        high = solved[p].astype(jnp.bfloat16).astype(jnp.float32)
        middle = (solved[p] - high).astype(jnp.bfloat16).astype(jnp.float32)
        low = solved[p] - high - middle
        stacked = jnp.where(
            split_rows == 0,
            high,
            jnp.where(split_rows == 1, middle, jnp.where(split_rows == 2, low, 0.0)),
        )
        split.append(stacked.astype(jnp.bfloat16))

    span = rows_here // ranks
    ready = 0
    for rank in range(ranks):
        while ready < parts and ready * width < (rank + 1) * span:
            copies[ready].wait()
            ready += 1
        fitted = jnp.zeros((16, span), jnp.float32)
        for p in range(2):
            fitted = fitted + jnp.dot(
                split[p],
                design[p, :, rank * span : (rank + 1) * span],
                preferred_element_type=jnp.float32,
            )
        fitted = jnp.sum(fitted, axis=0, keepdims=True)
        for line in range(lines):
            share_ref[rank, line : line + 1, :] = fitted[:, line * 128 : line * 128 + 128]


def finish_kernel(
    n,
    root_total,
    share_ref,
    arc_ref,
    value_ref,
    target_ref,
    residual_ref,
    bias_ref,
    landed,
    send,
    recv,
):
    me = lax.axis_index("ord")
    barrier = pltpu.get_barrier_semaphore()

    def greet(k, _):
        pl.semaphore_signal(
            barrier, inc=1, device_id={"ord": lax.rem(me + k, n)}, device_id_type=MESH
        )
        return 0

    lax.fori_loop(1, n, greet, 0)
    pl.semaphore_wait(barrier, n - 1)

    def scatter(k):
        peer = lax.rem(me + k, n)
        return pltpu.make_async_remote_copy(
            src_ref=share_ref.at[peer],
            dst_ref=landed.at[k],
            send_sem=send.at[k],
            recv_sem=recv.at[k],
            device_id={"ord": peer},
            device_id_type=MESH,
        )

    def start(k, _):
        scatter(k).start()
        return 0

    lax.fori_loop(1, n, start, 0)

    def add(k, summed):
        scatter(k).wait_recv()
        return summed + landed[k]

    summed = lax.fori_loop(1, n, add, share_ref[me]) / root_total
    lines = arc_ref.shape[0]
    bias = (target_ref[0:1, :] - summed[lines : lines + 1, :]) / target_ref[1:2, :]
    bias_ref[...] = bias
    arcs = arc_ref[...]
    bias_rows = jnp.zeros(arcs.shape, jnp.float32)
    for k in range(ARC_DEV):
        bias_rows = bias_rows + jnp.where(arcs == k, bias[:, k : k + 1], 0.0)
    residual_ref[...] = jnp.where(
        arcs < ARC_DEV, value_ref[...] - summed[0:lines, :] - bias_rows, 0.0
    )

    def end(k, _):
        scatter(k).wait_send()
        return 0

    lax.fori_loop(1, n, end, 0)


def per_device(obs_colat, obs_lon, obs_value, obs_arc, reg_weight):
    rows_here = obs_colat.shape[0]
    arc_devices = lax.axis_size("arc")
    order_devices = lax.axis_size("ord")
    total_rows = rows_here * arc_devices
    ord_me = lax.axis_index("ord")
    first_order = ord_me * 2 + jnp.arange(2, dtype=jnp.int32)
    grid_shape = (rows_here // 128, 128)
    steps = rows_here // CHUNK

    orders = jnp.concatenate([first_order, DEG - first_order])
    order_float = orders.astype(jnp.float32)[:, None, None]
    log_coeff = jnp.take(jnp.asarray(log_sectoral()), orders)[:, None, None]
    colat = obs_colat.reshape(grid_shape)
    lon = obs_lon.reshape(grid_shape)
    arcs = obs_arc.reshape(grid_shape)
    value = jnp.where(arcs < ARC_DEV, obs_value.reshape(grid_shape).astype(jnp.float32), 0.0)
    cosine = jnp.cos(colat)
    sectoral = jnp.exp(order_float * jnp.log(jnp.sin(colat))[None] + log_coeff)
    seeds = jnp.where(
        (arcs < ARC_DEV)[None], sectoral * jnp.cos(order_float * lon[None]), 0.0
    )
    member = jnp.arange(ARC_DEV, dtype=jnp.int32)[:, None] == obs_arc[None, :]
    counts = jnp.sum(member.astype(jnp.float32), axis=1)
    table = jnp.asarray(recursion_table(2 * order_devices).reshape(order_devices, -1))
    coef = lax.dynamic_index_in_dim(table, ord_me, keepdims=False)

    lines = CHUNK // 128
    design, normal, sums = pl.pallas_call(
        design_kernel,
        grid=(steps,),
        in_specs=[
            pl.BlockSpec(memory_space=pltpu.SMEM),
            pl.BlockSpec((lines, 128), lambda i: (i, 0)),
            pl.BlockSpec((4, lines, 128), lambda i: (0, i, 0)),
            pl.BlockSpec((lines, 128), lambda i: (i, 0)),
            pl.BlockSpec((ARC_DEV, CHUNK), lambda i: (0, i)),
            pl.BlockSpec((ARC_DEV, 128), lambda i: (0, 0)),
        ],
        out_specs=[
            pl.BlockSpec((2, ROWS, CHUNK), lambda i: (0, 0, i)),
            pl.BlockSpec((2, WIDE, WIDE), lambda i: (0, 0, 0)),
            pl.BlockSpec((2, ARC_DEV, WIDE), lambda i: (0, 0, 0)),
        ],
        out_shape=[
            jax.ShapeDtypeStruct((2, ROWS, rows_here), jnp.bfloat16),
            jax.ShapeDtypeStruct((2, WIDE, WIDE), jnp.float32),
            jax.ShapeDtypeStruct((2, ARC_DEV, WIDE), jnp.float32),
        ],
        scratch_shapes=[
            pltpu.VMEM((2 * TILES * WIDE, 128), jnp.float32),
            pltpu.VMEM((2, ROWS, WIDE), jnp.float32),
        ],
        compiler_params=pltpu.CompilerParams(vmem_limit_bytes=48 * MIB),
        name="design_normals",
    )(
        coef,
        cosine,
        seeds,
        value,
        member.astype(jnp.bfloat16),
        jnp.broadcast_to(counts[:, None], (ARC_DEV, 128)),
    )

    rows_each = 2 * WIDE // arc_devices
    summed = pl.pallas_call(
        functools.partial(reduce_kernel, arc_devices),
        in_specs=[pl.BlockSpec(memory_space=pltpu.VMEM)],
        out_specs=pl.BlockSpec(memory_space=pltpu.VMEM),
        out_shape=jax.ShapeDtypeStruct((arc_devices, rows_each, WIDE), jnp.float32),
        scratch_shapes=[pltpu.VMEM((arc_devices, rows_each, WIDE), jnp.float32)]
        + [pltpu.SemaphoreType.DMA((arc_devices,))] * 4,
        compiler_params=pltpu.CompilerParams(collective_id=0, has_side_effects=True),
        name="reduce_normals",
    )(normal.reshape(arc_devices, rows_each, WIDE))

    share_lines = rows_here // order_devices // 128
    parts = 4
    regular = jnp.concatenate(
        [reg_weight, jnp.ones((2, WIDE - BLOCK), jnp.float32)], axis=1
    ).reshape(2, 1, WIDE)
    solved, share = pl.pallas_call(
        functools.partial(solve_kernel, total_rows, parts=parts),
        in_specs=[
            pl.BlockSpec(memory_space=pltpu.VMEM),
            pl.BlockSpec(memory_space=pltpu.VMEM),
            pl.BlockSpec(memory_space=pltpu.VMEM),
            pl.BlockSpec(memory_space=pl.ANY),
        ],
        out_specs=[
            pl.BlockSpec(memory_space=pltpu.VMEM),
            pl.BlockSpec(memory_space=pltpu.VMEM),
        ],
        out_shape=[
            jax.ShapeDtypeStruct((2, WIDE), jnp.float32),
            jax.ShapeDtypeStruct((order_devices, 16, 128), jnp.float32),
        ],
        scratch_shapes=[
            pltpu.VMEM((2, WIDE, rows_here), jnp.bfloat16),
            pltpu.VMEM((2, WIDE, WIDE), jnp.float32),
            pltpu.SemaphoreType.DMA((parts,)),
        ],
        compiler_params=pltpu.CompilerParams(vmem_limit_bytes=48 * MIB),
        name="solve_fit",
    )(summed.reshape(2, WIDE, WIDE), regular, sums, design)

    local_arcs = lax.dynamic_slice_in_dim(arcs, ord_me * share_lines, share_lines)
    local_value = lax.dynamic_slice_in_dim(value, ord_me * share_lines, share_lines)
    target = jnp.stack([sums[0, :, VALUE_ROW], counts])
    target = jnp.pad(target, ((0, 6), (0, 128 - ARC_DEV)), constant_values=1.0)
    residual, bias = pl.pallas_call(
        functools.partial(finish_kernel, order_devices, math.sqrt(total_rows)),
        in_specs=[pl.BlockSpec(memory_space=pltpu.VMEM)] * 4,
        out_specs=[pl.BlockSpec(memory_space=pltpu.VMEM)] * 2,
        out_shape=[
            jax.ShapeDtypeStruct((share_lines, 128), jnp.float32),
            jax.ShapeDtypeStruct((1, 128), jnp.float32),
        ],
        scratch_shapes=[pltpu.VMEM((order_devices, 16, 128), jnp.float32)]
        + [pltpu.SemaphoreType.DMA((order_devices,))] * 2,
        compiler_params=pltpu.CompilerParams(collective_id=1, has_side_effects=True),
        name="exchange_fit",
    )(share, local_arcs, local_value, target)

    return (solved[:, :BLOCK], bias[0, :ARC_DEV], residual.reshape(-1))


def solution(mesh):
    placed = (P("arc"), P("arc"), P("arc"), P("arc"), P("ord", None))
    return jax.shard_map(
        per_device,
        mesh=mesh,
        in_specs=placed,
        out_specs=(P("ord", None), P("arc"), P(("arc", "ord"))),
        check_vma=False,
    )
```

time: 1020 us -> 160 us (0.16)
  other arithmetic: 554 us -> 4.56 us
  matrix products: 154 us -> 0 us
  Pallas kernels: 0 us -> 144 us
  waiting for transfers between devices: 116 us -> 0 us
  local copies, waits for them, and re-layouts: 106 us -> 9.65 us
  blocking collectives: 62.6 us -> 0 us
  between operations: 14.6 us -> 0.74 us
    mul x63 -> x0, other arithmetic: 246 us -> none  [recurse(): emitted = jnp.where((degree <= DEG)[:, None], current, 0.0) * phases]
    le x21 -> x0, other arithmetic: 158 us -> none  [recurse(): emitted = jnp.where((degree <= DEG)[:, None], current, 0.0) * phases]
    dot_general x9 -> x0, matrix products: 151 us -> none  [the longest x2 54.8 us: fit_rows(): jnp.dot(solution[pair_index], columns[:, pair_index, :].astype(jnp.float3...]
    pallas_call x0 -> x4, Pallas kernels: none -> 144 us  [the longest x1 76.8 us: per_device(): pl.pallas_call(design_kernel, grid=(steps,), in_specs=[pl.BlockSpec(memor...]
    psum x2 -> x0, waiting for transfers between devices: 116 us -> none  [the longest x1 116 us: per_device(): fitted = lax.psum(partial_fit, 'ord') / root_total]
    another operation x19 -> x1, other arithmetic: 106 us -> 0.61 us  [per_device(): target = jnp.stack([sums[0, :, VALUE_ROW], counts])]
    psum x1 -> x0, blocking collectives: 62.6 us -> none  [per_device(): normal_sum, right_sum = lax.psum((normal_part, right_part), 'arc')]
    slice x22 -> x1, local copies, waits for them, and re-layouts: 61.1 us -> 0.18 us  [per_device(): target = jnp.stack([sums[0, :, VALUE_ROW], counts])]
  transfers between devices with their start and end apart: 2 -> 0, of which waited for: 1 -> 0; matrix products, arithmetic and copies ran while one was open for 7% -> 0% of each run, Pallas kernels for 0% -> 0%
where the time goes in v1:
time: 160 us; the launch traced here: 159 us
  Pallas kernels  144 us (90%)
  local copies, waits for them, and re-layouts  9.65 us (6%)
  other arithmetic  4.56 us (3%)
    pallas_call x1, Pallas kernels, per_device(): pl.pallas_call(design_kernel, grid=(steps,), in_specs=[pl.BlockSpec(memor...  76.8 us
    pallas_call x1, Pallas kernels, per_device(): pl.pallas_call(functools.partial(solve_kernel, total_rows, parts=parts),...  27.7 us
    pallas_call x1, Pallas kernels, per_device(): pl.pallas_call(functools.partial(reduce_kernel, arc_devices), in_specs=[p...  24.4 us
    pallas_call x1, Pallas kernels, per_device(): pl.pallas_call(functools.partial(finish_kernel, order_devices, math.sqrt(...  15.6 us
    unnamed x11, local copies, waits for them, and re-layouts  3.76 us

profile of v1, /device:TPU:1, one launch (start us, length us, event | category | flops | bytes accessed | tf_op | source)
XLA Modules:
  0.0 159.4 jit_solution(14624144596482169950)
XLA Ops:
  0.6 0.0 copy-start.3
  0.7 0.1 fusion.1
  0.7 1.3 gather_fusion
  2.1 0.1 and_select_fusion
  2.1 0.1 fusion.3
  2.2 1.2 log_bitcast_fusion
  3.5 0.9 convert_select_fusion
  4.4 2.3 %multiply_select_fusion.seed_ref = f32[4,192,128]{2,1,0:T(8,128)S(1)} fusion(f32[192,128]{1,0:T(8,128)} %bitcast.30, f32[4]{0:T(128)S(1)} %and_select_fusion, f32[192,128]{1,0:T(8,128)S(1)} %get-tuple-element.19, f32[4]{0:T(128)S(1)} %fusion.3, pred[192,128]{1,0:T(8,128)(4,1)S(1)} %get-tuple-element.18), kind=kLoop, calls=%fused_computation.4 | loop fusion | flops 491520 | bytes 614432 | tf_op jit(solution)/shard_map/jit(_where)/select_n | solution.py:448
  6.7 0.8 constant_dynamic-slice_fusion.2
  7.5 0.0 copy-done.3
  7.5 0.3 convert_reduce_fusion
  7.8 0.1 broadcast_in_dim.33.counts_ref
  7.9 0.0 copy-start.4
  7.9 0.1 fusion.member_ref
  8.0 76.8 %design_normals.1 = (bf16[2,272,24576]{2,1,0:T(8,128)(2,1)}, f32[2,256,256]{2,1,0:T(8,128)S(1)}, f32[2,16,256]{2,1,0:T(8,128)S(1)}) custom-call(f32[1024]{0:T(1024)S(1)} %bitcast.28, f32[192,128]{1,0:T(8,128)S(1)} %get-tuple-element.20.t_ref, f32[4,192,128]{2,1,0:T(8,128)S(1)} %multiply_select_fusion.seed_ref, f32[192,128]{1,0:T(8,128)S(1)} %get-tuple-element.17.value_ref, ...), custom_call_target="tpu_custom_call" | custom-call | tf_op jit(solution)/shard_map/design_normals/pallas_call | solution.py:457
  84.8 0.0 copy-start.1
  84.8 0.8 copy-done.1
  85.6 24.4 %reduce_normals.1 = f32[16,32,256]{2,1,0:T(8,128)} custom-call(f32[16,32,256]{2,1,0:T(8,128)} %bitcast.27), custom_call_target="tpu_custom_call" | custom-call | tf_op jit(solution)/shard_map/reduce_normals/pallas_call | solution.py:494
  110.0 0.0 copy-done.4
  110.0 0.0 copy-start
  110.0 1.0 copy-done
  111.1 27.7 %solve_fit.1 = (f32[2,256]{1,0:T(2,128)}, f32[16,16,128]{2,1,0:T(8,128)S(1)}) custom-call(f32[2,256,256]{2,1,0:T(8,128)S(1)} %bitcast.26, f32[2,1,256]{2,1,0:T(1,128)S(1)} %reshape.158.regular_ref, f32[2,16,256]{2,1,0:T(8,128)S(1)} %get-tuple-element.11.sums_ref, bf16[2,272,24576]{2,1,0:T(8,128)(2,1)} %get-tuple-element.12.design_hbm), custom_call_target="tpu_custom_call" | custom-call | tf_op jit(solution)/shard_map/solve_fit/pallas_call | solution.py:510
  138.8 0.0 copy-start.2
  138.8 0.6 copy-done.2
  139.4 0.2 slice_reduce_fusion
  139.6 0.6 select_maximum_fusion.target_ref
  140.2 0.6 constant_dynamic-slice_fusion.value_ref
  140.8 0.6 constant_dynamic-slice_fusion.1.arc_ref
  141.4 15.6 %exchange_fit.1 = (f32[12,128]{1,0:T(8,128)}, f32[1,128]{1,0:T(1,128)}) custom-call(f32[16,16,128]{2,1,0:T(8,128)} %copy-done.2, s32[12,128]{1,0:T(8,128)} %constant_dynamic-slice_fusion.1.arc_ref, f32[12,128]{1,0:T(8,128)} %constant_dynamic-slice_fusion.value_ref, f32[8,128]{1,0:T(8,128)} %select_maximum_fusion.target_ref), custom_call_target="tpu_custom_call" | custom-call | tf_op jit(solution)/shard_map/exchange_fit/pallas_call | solution.py:539
  157.0 1.1 slice_bitcast_fusion
  158.1 1.3 copy.11
  (5 shorter events, 0.0 us)
Async XLA Ops:
  0.6 6.9 %copy-start.3 = (s32[24576]{0:T(1024)S(1)}, s32[24576]{0:T(1024)}, u32[]{:S(2)}) copy-start(s32[24576]{0:T(1024)} %param.10) | copy-start | bytes 294916
  7.9 102.1 %copy-start.4 = (f32[2,252]{1,0:T(2,128)S(1)}, f32[2,252]{1,0:T(2,128)}, u32[]{:S(2)}) copy-start(f32[2,252]{1,0:T(2,128)} %param.11) | copy-start | bytes 6052
  84.8 0.8 copy-start.1
  110.0 1.0 copy-start
  138.8 0.6 copy-start.2

commit v2 on v0

v2 whole, which is shorter than its diff:
```python
import math

import jax
import jax.numpy as jnp
import numpy as np
from jax import lax
from jax.experimental import pallas as pl
from jax.experimental.pallas import tpu as pltpu
from jax.sharding import PartitionSpec as P

DEG = 250
BLOCK = 252
ARC_DEV = 16
WIDE = 256
ROWS = WIDE + ARC_DEV
VALUE_ROW = 255
COUNT_ROW = 254
STRIDE = 20
HALF_PI = float(np.float32(0.5 * math.pi))
HALF_PI_REST = 0.5 * math.pi - HALF_PI
COSINE = [(-1.0) ** k * (2.0 * math.pi) ** (2 * k) / math.factorial(2 * k) for k in range(11)]
CHUNK = 4096
TILES = CHUNK // 128
GROUPS = CHUNK // 1024
PANEL = 64
EACH = 32
LINES = 12
MESH = pl.DeviceIdType.MESH
MIB = 1024 * 1024
HIGHEST = lax.Precision.HIGHEST


def log_sectoral():
    increments = [0.0, 0.5 * math.log(3.0)] + [
        0.5 * math.log((2.0 * degree_now + 1.0) / (2.0 * degree_now))
        for degree_now in range(2, DEG + 1)
    ]
    return np.cumsum(np.array(increments[: DEG + 1])).astype(np.float32)


def recursion_table(pairs):
    table = np.zeros((pairs, 2, WIDE), np.float64)
    table[:, 1, COUNT_ROW:] = -1.0
    for pair in range(pairs):
        for column in range(BLOCK):
            low = column < DEG + 1 - pair
            order = pair if low else DEG - pair
            degree = pair + column if low else column - 1
            if degree == order:
                table[pair, 0, column] = 0.0
                table[pair, 1, column] = -1.0
                continue
            denominator = float((degree - order) * (degree + order))
            table[pair, 0, column] = math.sqrt(
                (2.0 * degree - 1.0) * (2.0 * degree + 1.0) / denominator
            )
            table[pair, 1, column] = math.sqrt(
                max((2.0 * degree + 1.0) * (degree + order - 1.0) * (degree - order - 1.0), 0.0)
                / (denominator * max(2.0 * degree - 3.0, 1.0))
            )
    logs = log_sectoral()
    table = table.reshape(pairs // 2, 4 * WIDE)
    names = [
        [logs[q] for q in (2 * z, 2 * z + 1, DEG - 2 * z, DEG - 1 - 2 * z)]
        for z in range(pairs // 2)
    ]
    return np.concatenate([table, np.array(names), np.zeros((pairs // 2, 4))], 1).astype(
        np.float32
    )


def circle(turns, order):
    angle = turns * order
    angle = angle - jnp.floor(angle + 0.5)
    square = angle * angle
    result = jnp.full_like(square, COSINE[-1])
    for coefficient in COSINE[-2::-1]:
        result = result * square + coefficient
    return result


def polar(colat):
    x = (colat - HALF_PI) - HALF_PI_REST
    square = x * x
    odd = jnp.full_like(square, 1.0 / math.factorial(15))
    odd = -odd
    even = jnp.full_like(square, 1.0 / math.factorial(16))
    for k in range(6, -1, -1):
        odd = odd * square + (-1.0) ** k / math.factorial(2 * k + 1)
        even = even * square + (-1.0) ** (k + 1) / math.factorial(2 * k + 2)
    return -(odd * x), even * square + 1.0


def make_normals(first_pair, chunks, coef_ref, colat, lon, value, arcs, kept, design, scratch):
    window0, window1, starting, total = scratch
    starts = [DEG + 1 - first_pair, DEG - first_pair]
    chains = [(p, v) for p in range(2) for v in range(GROUPS)]
    orders = [first_pair, first_pair + 1, DEG - first_pair, DEG - 1 - first_pair]
    orders = [order.astype(jnp.float32) for order in orders]
    total[...] = jnp.zeros_like(total)
    window1[...] = jnp.zeros_like(window1)

    def chunk_body(chunk, _):
        line = pl.multiple_of(chunk * TILES, TILES)
        first_lane = pl.multiple_of(chunk * CHUNK, CHUNK)
        t = []
        for v in range(GROUPS):
            rows = pl.ds(pl.multiple_of(line + v * 8, 8), 8)
            cosine, sine = polar(colat[rows, :])
            t.append(cosine)
            log_sine = jnp.log(sine)
            turns = lon[rows, :] * (0.5 / math.pi)
            valid = arcs[rows, :] < ARC_DEV
            for q in range(4):
                sectoral = jnp.exp(orders[q] * log_sine + coef_ref[4 * WIDE + q])
                starting[q * TILES + v * 8 : q * TILES + v * 8 + 8, :] = jnp.where(
                    valid, sectoral * circle(turns, orders[q]), 0.0
                )
        kept[pl.ds(line, TILES), :] = jnp.where(
            arcs[pl.ds(line, TILES), :] < ARC_DEV,
            value[pl.ds(line, TILES), :].astype(jnp.float32),
            0.0,
        )

        def seed(q, v):
            return starting[q * TILES + v * 8 : q * TILES + v * 8 + 8, :]

        def extra(v, is_value):
            rows = pl.ds(pl.multiple_of(line + v * 8, 8), 8)
            if is_value:
                return kept[rows, :]
            return jnp.where(arcs[rows, :] < ARC_DEV, 1.0, 0.0)

        def convert(window, row):
            row = pl.multiple_of(row, 16)
            for p in range(2):
                for tile in range(TILES):
                    source = (p * TILES + tile) * STRIDE
                    lane = pl.multiple_of(first_lane + tile * 128, 128)
                    design[p, pl.ds(row, 16), pl.ds(lane, 128)] = window[
                        source : source + 16, :
                    ].astype(jnp.bfloat16)

        def columns16(window, base, carried, turning, last):
            previous, before = carried
            for inner in range(16):
                column = base + inner
                rising = [coef_ref[p * 2 * WIDE + column] for p in range(2)]
                falling = [coef_ref[p * 2 * WIDE + WIDE + column] for p in range(2)]
                current = []
                for i, (p, v) in enumerate(chains):
                    older = before[i]
                    if turning:
                        older = jnp.where(column == starts[p], seed(2 + p, v), older)
                    if last and inner >= 14:
                        older = jnp.where(
                            column == WIDE - 16 + inner, extra(v, inner == 15), older
                        )
                    now = rising[p] * (t[v] * previous[i]) - falling[p] * older
                    window[pl.ds((p * TILES + v * 8) * STRIDE + inner, 8, stride=STRIDE), :] = now
                    current.append(now)
                before, previous = previous, tuple(current)
            return previous, before

        def columns32(block, carried, turning):
            base = block * 32
            convert(window1, lax.rem(base + (WIDE - 16), WIDE))
            carried = columns16(window0, base, carried, turning, False)
            convert(window0, base)
            return columns16(window1, base + 16, carried, turning, True)

        zeros = tuple(jnp.zeros((8, 128), jnp.float32) for _ in chains)
        carried = (zeros, tuple(seed(p, v) for p, v in chains))
        turn = starts[0] // 32
        carried = lax.fori_loop(0, turn, lambda block, c: columns32(block, c, False), carried)
        carried = columns32(turn, carried, True)
        lax.fori_loop(turn + 1, WIDE // 32, lambda block, c: columns32(block, c, False), carried)
        convert(window1, WIDE - 16)

        arc_names = lax.broadcasted_iota(jnp.int32, (ARC_DEV, 128), 0)
        for tile in range(TILES):
            member = arc_names == arcs[pl.ds(line + tile, 1), :]
            member = jnp.where(member, 1.0, 0.0).astype(jnp.bfloat16)
            lane = pl.multiple_of(first_lane + tile * 128, 128)
            for p in range(2):
                design[p, WIDE:ROWS, pl.ds(lane, 128)] = member

        for p in range(2):
            total[p] += lax.dot_general(
                design[p, :, pl.ds(first_lane, CHUNK)],
                design[p, 0:WIDE, pl.ds(first_lane, CHUNK)],
                (((1,), (1,)), ((), ())),
                preferred_element_type=jnp.float32,
            )
        return 0

    lax.fori_loop(0, chunks, chunk_body, 0)


def pack_normals(total, packed):
    row_ids = lax.broadcasted_iota(jnp.int32, (128, 128), 0)
    column_ids = lax.broadcasted_iota(jnp.int32, (128, 128), 1)
    for p in range(2):
        sums = total[p, WIDE:ROWS, :]
        scaled = sums / sums[:, COUNT_ROW : COUNT_ROW + 1]
        normal = total[p, 0:WIDE, :] - lax.dot_general(
            scaled,
            sums,
            (((0,), (0,)), ((), ())),
            precision=HIGHEST,
            preferred_element_type=jnp.float32,
        )
        corner = normal[128:WIDE, 128:WIDE]
        diagonal = jnp.sum(jnp.where(row_ids == column_ids, corner, 0.0), axis=0, keepdims=True)
        packed[p * WIDE : p * WIDE + 128, :] = jnp.where(
            row_ids == BLOCK - 128, diagonal, normal[128:WIDE, 0:128]
        )
        packed[p * WIDE + 128 : p * WIDE + WIDE, :] = jnp.where(
            row_ids >= column_ids, normal[0:128, 0:128], corner
        )


def remote(axis, peer, source, target, send, recv):
    return pltpu.make_async_remote_copy(
        src_ref=source,
        dst_ref=target,
        send_sem=send,
        recv_sem=recv,
        device_id={axis: peer},
        device_id_type=MESH,
    )


def each(first, last, action):
    def body(k, _):
        action(k)
        return 0

    lax.fori_loop(first, last, body, 0)


def reduce_normals(n, packed, summed, landed, send1, recv1, send2, recv2):
    me = lax.axis_index("arc")

    def part(owner):
        return pl.ds(pl.multiple_of(owner * EACH, EACH), EACH)

    def scatter(k):
        peer = lax.rem(me + k, n)
        return remote(
            "arc", peer, packed.at[part(peer)], landed.at[k], send1.at[k], recv1.at[k]
        )

    def gather(k, owner):
        peer = lax.rem(me + k, n)
        return remote(
            "arc", peer, summed.at[part(owner)], summed.at[part(owner)], send2.at[k], recv2.at[k]
        )

    each(1, n, lambda k: scatter(k).start())

    def add(k, mine):
        scatter(k).wait_recv()
        return mine + landed[k]

    summed[part(me), :] = lax.fori_loop(1, n, add, packed[part(me), :])
    each(1, n, lambda k: gather(k, me).start())
    each(1, n, lambda k: gather(k, lax.rem(me - k + n, n)).wait_recv())

    def end():
        each(1, n, lambda k: scatter(k).wait_send())
        each(1, n, lambda k: gather(k, me).wait_send())

    return end


def build_matrix(first_pair, total_rows, summed, regular_ref, work):
    row_ids = lax.broadcasted_iota(jnp.int32, (WIDE, WIDE), 0)
    column_ids = lax.broadcasted_iota(jnp.int32, (WIDE, WIDE), 1)
    regular = jnp.concatenate(
        [regular_ref[...], jnp.ones((2, WIDE - BLOCK), jnp.float32)], axis=1
    )
    eye = row_ids == column_ids
    for p in range(2):
        left_block = summed[p * WIDE : p * WIDE + 128, :]
        mixed = summed[p * WIDE + 128 : p * WIDE + WIDE, :]
        flipped = mixed.T
        below = row_ids[0:128, 0:128] > column_ids[0:128, 0:128]
        level = eye[0:128, 0:128]
        corner = jnp.where(below, flipped, mixed)
        corner = jnp.where(level, left_block[BLOCK - 128 : BLOCK - 127, :], corner)
        upper = jnp.concatenate(
            [jnp.where(below | level, mixed, flipped), left_block.T], axis=1
        )
        normal = jnp.concatenate([upper, jnp.concatenate([left_block, corner], axis=1)], axis=0)
        border = DEG + 1 - first_pair - p
        real = (row_ids < BLOCK) & (column_ids < BLOCK)
        same = ((row_ids < border) == (column_ids < border)) & real
        matrix = jnp.where(same, normal / total_rows, 0.0)
        matrix = matrix + jnp.where(
            eye & real, regular[p : p + 1, :], jnp.where(eye, 1.0, 0.0)
        )
        right = jnp.where(row_ids < BLOCK, normal / math.sqrt(total_rows), 0.0)
        work[p] = jnp.where(column_ids == VALUE_ROW, right, matrix)


def eliminate(work):
    for panel in range(WIDE // PANEL):
        top = panel * PANEL
        left = top // 128 * 128
        blocks = [work[p, top : top + PANEL, left:WIDE] for p in range(2)]
        panel_rows = lax.broadcasted_iota(jnp.int32, (PANEL, WIDE - left), 0)
        for k in range(min(PANEL, VALUE_ROW - top)):
            lane = top - left + k
            for p in range(2):
                block = blocks[p]
                row = block[k : k + 1, :]
                inverse = 1.0 / block[k : k + 1, lane : lane + 1]
                scaled = row * inverse
                updated = block - block[:, lane : lane + 1] * scaled
                blocks[p] = jnp.where(panel_rows == k, scaled, updated)
        for p in range(2):
            inner = top % 128
            weights = blocks[p]
            pieces = []
            if inner > 0:
                pieces.append(jnp.zeros((inner, WIDE - left), jnp.float32))
            pieces.append(weights)
            if inner + PANEL < 128:
                pieces.append(jnp.zeros((128 - inner - PANEL, WIDE - left), jnp.float32))
            tall = jnp.concatenate(pieces, axis=0) if len(pieces) > 1 else weights
            factor = work[p, :, left : left + 128]
            if panel == WIDE // PANEL - 1:
                lanes = lax.broadcasted_iota(jnp.int32, (WIDE, 128), 1)
                factor = jnp.where(lanes == VALUE_ROW - left, 0.0, factor)
            work[p, :, left:WIDE] = work[p, :, left:WIDE] - jnp.dot(
                factor, tall, precision=HIGHEST, preferred_element_type=jnp.float32
            )
            work[p, top : top + PANEL, left:WIDE] = weights


def read_answer(work):
    row_ids = lax.broadcasted_iota(jnp.int32, (WIDE, WIDE), 0)
    column_ids = lax.broadcasted_iota(jnp.int32, (WIDE, WIDE), 1)
    solved = []
    for p in range(2):
        answer = jnp.where(
            row_ids == column_ids, work[p, :, VALUE_ROW : VALUE_ROW + 1], 0.0
        )
        answer = jnp.sum(answer, axis=0, keepdims=True)
        lanes = lax.broadcasted_iota(jnp.int32, (1, WIDE), 1)
        solved.append(jnp.where(lanes < BLOCK, answer, 0.0))
    return solved


def split_three(row):
    split_rows = lax.broadcasted_iota(jnp.int32, (16, WIDE), 0)
    high = row.astype(jnp.bfloat16).astype(jnp.float32)
    middle = (row - high).astype(jnp.bfloat16).astype(jnp.float32)
    low = row - high - middle
    stacked = jnp.where(
        split_rows == 0,
        high,
        jnp.where(split_rows == 1, middle, jnp.where(split_rows == 2, low, 0.0)),
    )
    return stacked.astype(jnp.bfloat16)


def whole_kernel(
    arc_devices,
    order_devices,
    rows_here,
    coef_ref,
    colat_hbm,
    lon_hbm,
    value_hbm,
    arc_hbm,
    regular_ref,
    solution_ref,
    bias_ref,
    residual_ref,
    colat,
    lon,
    value,
    arcs,
    kept,
    design,
    window0,
    window1,
    starting,
    total,
    packed,
    summed,
    landed,
    work,
    share,
    arrived,
    loaded,
    send1,
    recv1,
    send2,
    recv2,
    send3,
    recv3,
):
    total_rows = rows_here * arc_devices
    root_total = math.sqrt(total_rows)
    ord_me = lax.axis_index("ord")
    arc_me = lax.axis_index("arc")
    first_pair = ord_me * 2
    loads = []
    for i, (far, near) in enumerate(
        [(colat_hbm, colat), (lon_hbm, lon), (value_hbm, value), (arc_hbm, arcs)]
    ):
        load = pltpu.make_async_copy(far, near, loaded.at[i])
        load.start()
        loads.append(load)

    barrier = pltpu.get_barrier_semaphore()

    def greet(axis, me, n):
        each(
            1,
            n,
            lambda k: pl.semaphore_signal(
                barrier, inc=1, device_id={axis: lax.rem(me + k, n)}, device_id_type=MESH
            ),
        )

    greet("arc", arc_me, arc_devices)
    greet("ord", ord_me, order_devices)
    share[...] = jnp.zeros_like(share)
    for load in loads:
        load.wait()

    make_normals(
        first_pair,
        rows_here // CHUNK,
        coef_ref,
        colat,
        lon,
        value,
        arcs,
        kept,
        design,
        (window0, window1, starting, total),
    )
    pack_normals(total, packed)
    pl.semaphore_wait(barrier, arc_devices + order_devices - 2)
    end_reduce = reduce_normals(arc_devices, packed, summed, landed, send1, recv1, send2, recv2)
    build_matrix(first_pair, total_rows, summed, regular_ref, work)
    eliminate(work)
    solved = read_answer(work)

    square = (ARC_DEV, 128)
    corner = lax.broadcasted_iota(jnp.int32, square, 0) == lax.broadcasted_iota(
        jnp.int32, square, 1
    )
    offsets = jnp.zeros((ARC_DEV, 1), jnp.float32)
    for p in range(2):
        solution_ref[p : p + 1, :] = solved[p][:, 0:BLOCK]
        offsets = offsets + jnp.sum(total[p, WIDE:ROWS, :] * solved[p], axis=1, keepdims=True)
    offset_row = jnp.sum(jnp.where(corner, offsets, 0.0), axis=0, keepdims=True)
    split = [split_three(solved[p]) for p in range(2)]
    span = rows_here // order_devices

    def send_fit(k, source):
        peer = lax.rem(ord_me + k, order_devices)
        return remote("ord", peer, share.at[peer], arrived.at[source], send3.at[k], recv3.at[k])

    def fit(k):
        rank = lax.rem(ord_me + k, order_devices)
        lane = pl.multiple_of(rank * span, span)
        fitted = jnp.zeros((16, span), jnp.float32)
        for p in range(2):
            fitted = fitted + jnp.dot(
                split[p],
                design[p, 0:WIDE, pl.ds(lane, span)],
                preferred_element_type=jnp.float32,
            )
        fitted = jnp.sum(fitted, axis=0, keepdims=True)
        for line in range(LINES):
            share[rank, line : line + 1, :] = fitted[:, line * 128 : line * 128 + 128]
        share[rank, LINES : LINES + 1, :] = offset_row

    def fit_and_send(k):
        fit(k)
        send_fit(k, ord_me).start()

    each(1, order_devices, fit_and_send)
    fit(0)

    arrived[ord_me] = share[ord_me]
    each(
        1,
        order_devices,
        lambda k: send_fit(k, lax.rem(ord_me - k + order_devices, order_devices)).wait_recv(),
    )
    final = arrived[0]
    for source in range(1, order_devices):
        final = final + arrived[source]
    final = final / root_total
    counts = total[0, WIDE:ROWS, COUNT_ROW : COUNT_ROW + 1]
    target = total[0, WIDE:ROWS, VALUE_ROW : VALUE_ROW + 1]
    bias = jnp.where(corner, (target - final[LINES : LINES + 1, :]) / counts, 0.0)
    bias = jnp.sum(bias, axis=0, keepdims=True)
    bias_ref[...] = bias[:, 0:ARC_DEV]
    local = pl.ds(ord_me * LINES, LINES)
    my_arcs = arcs[local, :]
    bias_rows = jnp.zeros((LINES, 128), jnp.float32)
    for k in range(ARC_DEV):
        bias_rows = bias_rows + jnp.where(my_arcs == k, bias[:, k : k + 1], 0.0)
    residual_ref[...] = jnp.where(
        my_arcs < ARC_DEV, kept[local, :] - final[0:LINES, :] - bias_rows, 0.0
    )
    end_reduce()
    each(1, order_devices, lambda k: send_fit(k, ord_me).wait_send())


def per_device(obs_colat, obs_lon, obs_value, obs_arc, reg_weight):
    rows_here = obs_colat.shape[0]
    arc_devices = lax.axis_size("arc")
    order_devices = lax.axis_size("ord")
    lines = (rows_here // 128, 128)
    table = jnp.asarray(recursion_table(2 * order_devices))
    coef = lax.dynamic_index_in_dim(table, lax.axis_index("ord"), keepdims=False)

    def kernel(*refs):
        whole_kernel(arc_devices, order_devices, rows_here, *refs)

    vmem = pl.BlockSpec(memory_space=pltpu.VMEM)
    solved, bias, residual = pl.pallas_call(
        kernel,
        in_specs=[pl.BlockSpec(memory_space=pltpu.SMEM)]
        + [pl.BlockSpec(memory_space=pl.ANY)] * 4
        + [vmem],
        out_specs=[vmem] * 3,
        out_shape=[
            jax.ShapeDtypeStruct((2, BLOCK), jnp.float32),
            jax.ShapeDtypeStruct((1, ARC_DEV), jnp.float32),
            jax.ShapeDtypeStruct((LINES, 128), jnp.float32),
        ],
        scratch_shapes=[
            pltpu.VMEM(lines, jnp.float32),
            pltpu.VMEM(lines, jnp.float32),
            pltpu.VMEM(lines, jnp.bfloat16),
            pltpu.VMEM(lines, jnp.int32),
            pltpu.VMEM(lines, jnp.float32),
            pltpu.VMEM((2, ROWS, rows_here), jnp.bfloat16),
            pltpu.VMEM((2 * TILES * STRIDE, 128), jnp.float32),
            pltpu.VMEM((2 * TILES * STRIDE, 128), jnp.float32),
            pltpu.VMEM((4 * TILES, 128), jnp.float32),
            pltpu.VMEM((2, ROWS, WIDE), jnp.float32),
            pltpu.VMEM((2 * WIDE, 128), jnp.float32),
            pltpu.VMEM((2 * WIDE, 128), jnp.float32),
            pltpu.VMEM((arc_devices, EACH, 128), jnp.float32),
            pltpu.VMEM((2, WIDE, WIDE), jnp.float32),
            pltpu.VMEM((order_devices, 16, 128), jnp.float32),
            pltpu.VMEM((order_devices, 16, 128), jnp.float32),
            pltpu.SemaphoreType.DMA((4,)),
        ]
        + [pltpu.SemaphoreType.DMA((arc_devices,))] * 4
        + [pltpu.SemaphoreType.DMA((order_devices,))] * 2,
        compiler_params=pltpu.CompilerParams(
            collective_id=0, has_side_effects=True, vmem_limit_bytes=56 * MIB
        ),
        name="whole",
    )(
        coef,
        obs_colat.reshape(lines),
        obs_lon.reshape(lines),
        obs_value.reshape(lines),
        obs_arc.reshape(lines),
        reg_weight,
    )
    return (solved, bias.reshape(-1), residual.reshape(-1))


def solution(mesh):
    placed = (P("arc"), P("arc"), P("arc"), P("arc"), P("ord", None))
    return jax.shard_map(
        per_device,
        mesh=mesh,
        in_specs=placed,
        out_specs=(P("ord", None), P("arc"), P(("arc", "ord"))),
        check_vma=False,
    )
```

time: 1020 us -> 81.5 us (0.08); the launches traced: 1010 us -> 81.2 us
  other arithmetic: 554 us -> 0 us
  matrix products: 154 us -> 0 us
  waiting for transfers between devices: 116 us -> 0 us
  local copies, waits for them, and re-layouts: 106 us -> 3.74 us
  Pallas kernels: 0 us -> 76.8 us
  blocking collectives: 62.6 us -> 0 us
  between operations: 14.6 us -> 0.66 us
    mul x63 -> x0, other arithmetic: 246 us -> none  [recurse(): emitted = jnp.where((degree <= DEG)[:, None], current, 0.0) * phases]
    le x21 -> x0, other arithmetic: 158 us -> none  [recurse(): emitted = jnp.where((degree <= DEG)[:, None], current, 0.0) * phases]
    dot_general x9 -> x0, matrix products: 151 us -> none  [the longest x2 54.8 us: fit_rows(): jnp.dot(solution[pair_index], columns[:, pair_index, :].astype(jnp.float3...]
    psum x2 -> x0, waiting for transfers between devices: 116 us -> none  [the longest x1 116 us: per_device(): fitted = lax.psum(partial_fit, 'ord') / root_total]
    another operation x19 -> x0, other arithmetic: 106 us -> none  [the longest x10 66.2 us: solve_pairs(): factor = jnp.linalg.cholesky(matrix)]
    pallas_call x0 -> x1, Pallas kernels: none -> 76.8 us  [per_device(): pl.pallas_call(kernel, in_specs=[pl.BlockSpec(memory_space=pltpu.SMEM)] +...]
    psum x1 -> x0, blocking collectives: 62.6 us -> none  [per_device(): normal_sum, right_sum = lax.psum((normal_part, right_part), 'arc')]
    slice x22 -> x0, local copies, waits for them, and re-layouts: 61.1 us -> none  [the longest x1 46.5 us: fit_rows(): columns[:, pair_index, :].astype(jnp.float32)]
  transfers between devices with their start and end apart: 2 -> 0, of which waited for: 1 -> 0; matrix products, arithmetic and copies ran while one was open for 7% -> 0% of each run, Pallas kernels for 0% -> 0%
where the time goes in v2:
time: 81.5 us; the launch traced here: 81.2 us
  Pallas kernels  76.8 us (94%)
  local copies, waits for them, and re-layouts  3.74 us (5%)
    pallas_call x1, Pallas kernels, per_device(): pl.pallas_call(kernel, in_specs=[pl.BlockSpec(memory_space=pltpu.SMEM)] +...  76.8 us
    unnamed x7, local copies, waits for them, and re-layouts  2.35 us

profile of v2, /device:TPU:1, one launch (start us, length us, event | category | flops | bytes accessed | tf_op | source)
XLA Modules:
  0.0 81.2 jit_solution(13299074098586787009)
XLA Ops:
  0.6 1.4 %dynamic-slice_reduce_fusion.refs_0_ = f32[1032]{0:T(1024)} fusion(f32[16,1032]{1,0:T(8,128)} %constant.12.clone, s32[]{:T(128)S(6)} %select_n.4), kind=kLoop, calls=%fused_computation | loop fusion | bytes 8260 | tf_op jit(solution)/shard_map/jit(dynamic_index_in_dim)/dynamic_slice | solution.py:526
  2.0 76.8 %whole.1 = (f32[2,252]{1,0:T(2,128)}, f32[1,16]{1,0:T(1,128)}, f32[12,128]{1,0:T(8,128)}) custom-call(f32[1032]{0:T(1024)} %dynamic-slice_reduce_fusion.refs_0_, f32[192,128]{1,0:T(8,128)} %bitcast.6, f32[192,128]{1,0:T(8,128)} %bitcast.7, bf16[192,128]{1,0:T(8,128)(2,1)} %bitcast.9, s32[192,128]{1,0:T(8,128)} %bitcast.8, f32[2,252]{1,0:T(2,128)} %refs_5_.1), custom_call_target="tpu_custom_call" | custom-call | tf_op jit(solution)/shard_map/whole/pallas_call | solution.py:532
  78.9 0.0 copy-start
  78.9 0.0 copy-start.1
  78.9 1.2 %copy.12 = f32[2,252]{1,0:T(2,128)} copy(f32[2,252]{1,0:T(2,128)} %get-tuple-element.12) | data formatting | bytes 4032
  80.1 0.0 copy-done.1
  80.1 0.5 copy.13
  80.6 0.0 copy-done
  80.6 0.6 copy.14
Async XLA Ops:
  78.9 1.8 %copy-start = (f32[12,128]{1,0:T(8,128)S(1)}, f32[12,128]{1,0:T(8,128)}, u32[]{:S(2)}) copy-start(f32[12,128]{1,0:T(8,128)} %get-tuple-element.8) | copy-start | bytes 18436
  78.9 1.2 %copy-start.1 = (f32[1,16]{1,0:T(1,128)S(1)}, f32[1,16]{1,0:T(1,128)}, u32[]{:S(2)}) copy-start(f32[1,16]{1,0:T(1,128)} %get-tuple-element.7) | copy-start | bytes 196

commit v3 on v2

--- a/solution.py
+++ b/solution.py
@@ -19,7 +19,7 @@
 HALF_PI = float(np.float32(0.5 * math.pi))
 HALF_PI_REST = 0.5 * math.pi - HALF_PI
 COSINE = [(-1.0) ** k * (2.0 * math.pi) ** (2 * k) / math.factorial(2 * k) for k in range(11)]
-CHUNK = 4096
+CHUNK = 6144
 TILES = CHUNK // 128
 GROUPS = CHUNK // 1024
 PANEL = 64
@@ -59,14 +59,12 @@
                 / (denominator * max(2.0 * degree - 3.0, 1.0))
             )
     logs = log_sectoral()
-    table = table.reshape(pairs // 2, 4 * WIDE)
-    names = [
-        [logs[q] for q in (2 * z, 2 * z + 1, DEG - 2 * z, DEG - 1 - 2 * z)]
-        for z in range(pairs // 2)
-    ]
-    return np.concatenate([table, np.array(names), np.zeros((pairs // 2, 4))], 1).astype(
-        np.float32
-    )
+    result = np.zeros((pairs // 2, 8, WIDE), np.float32)
+    result[:, 0:4] = table.reshape(pairs // 2, 4, WIDE)
+    for z in range(pairs // 2):
+        for q, order in enumerate((2 * z, 2 * z + 1, DEG - 2 * z, DEG - 1 - 2 * z)):
+            result[z, 4, q] = logs[order]
+    return result
 
 
 def circle(turns, order):
@@ -91,18 +89,30 @@
     return -(odd * x), even * square + 1.0
 
 
-def make_normals(first_pair, chunks, coef_ref, colat, lon, value, arcs, kept, design, scratch):
+def make_normals(first_pair, halves, coef_ref, colat, lon, value, arcs, kept, designs, scratch):
     window0, window1, starting, total = scratch
     starts = [DEG + 1 - first_pair, DEG - first_pair]
     chains = [(p, v) for p in range(2) for v in range(GROUPS)]
     orders = [first_pair, first_pair + 1, DEG - first_pair, DEG - 1 - first_pair]
     orders = [order.astype(jnp.float32) for order in orders]
-    total[...] = jnp.zeros_like(total)
     window1[...] = jnp.zeros_like(window1)
-
-    def chunk_body(chunk, _):
-        line = pl.multiple_of(chunk * TILES, TILES)
-        first_lane = pl.multiple_of(chunk * CHUNK, CHUNK)
+    kept[...] = jnp.where(arcs[...] < ARC_DEV, value[...].astype(jnp.float32), 0.0)
+
+    def product(design, p, lane, width):
+        total[p] += lax.dot_general(
+            design[p, :, pl.ds(lane, width)],
+            design[p, 0:WIDE, pl.ds(lane, width)],
+            (((1,), (1,)), ((), ())),
+            preferred_element_type=jnp.float32,
+        )
+
+    def chunk_body(half, parity):
+        design, other = designs[parity], designs[1 - parity]
+        line = pl.multiple_of((2 * half + parity) * TILES, TILES)
+        first_lane = pl.multiple_of(half * CHUNK, CHUNK)
+        other_lane = first_lane
+        if parity == 0:
+            other_lane = lax.rem(half + halves - 1, halves) * CHUNK
         t = []
         for v in range(GROUPS):
             rows = pl.ds(pl.multiple_of(line + v * 8, 8), 8)
@@ -112,15 +122,10 @@
             turns = lon[rows, :] * (0.5 / math.pi)
             valid = arcs[rows, :] < ARC_DEV
             for q in range(4):
-                sectoral = jnp.exp(orders[q] * log_sine + coef_ref[4 * WIDE + q])
+                sectoral = jnp.exp(orders[q] * log_sine + coef_ref[4, q])
                 starting[q * TILES + v * 8 : q * TILES + v * 8 + 8, :] = jnp.where(
                     valid, sectoral * circle(turns, orders[q]), 0.0
                 )
-        kept[pl.ds(line, TILES), :] = jnp.where(
-            arcs[pl.ds(line, TILES), :] < ARC_DEV,
-            value[pl.ds(line, TILES), :].astype(jnp.float32),
-            0.0,
-        )
 
         def seed(q, v):
             return starting[q * TILES + v * 8 : q * TILES + v * 8 + 8, :]
@@ -145,8 +150,8 @@
             previous, before = carried
             for inner in range(16):
                 column = base + inner
-                rising = [coef_ref[p * 2 * WIDE + column] for p in range(2)]
-                falling = [coef_ref[p * 2 * WIDE + WIDE + column] for p in range(2)]
+                rising = [coef_ref[2 * p, column] for p in range(2)]
+                falling = [coef_ref[2 * p + 1, column] for p in range(2)]
                 current = []
                 for i, (p, v) in enumerate(chains):
                     older = before[i]
@@ -164,6 +169,8 @@
 
         def columns32(block, carried, turning):
             base = block * 32
+            quarter = CHUNK // 4
+            lane = pl.multiple_of(other_lane + lax.rem(block, 4) * quarter, quarter)
             convert(window1, lax.rem(base + (WIDE - 16), WIDE))
             carried = columns16(window0, base, carried, turning, False)
             convert(window0, base)
@@ -185,16 +192,15 @@
             for p in range(2):
                 design[p, WIDE:ROWS, pl.ds(lane, 128)] = member
 
-        for p in range(2):
-            total[p] += lax.dot_general(
-                design[p, :, pl.ds(first_lane, CHUNK)],
-                design[p, 0:WIDE, pl.ds(first_lane, CHUNK)],
-                (((1,), (1,)), ((), ())),
-                preferred_element_type=jnp.float32,
-            )
+    def two_chunks(half, _):
+        for parity in range(2):
+            chunk_body(half, parity)
+            for p in range(2):
+                product(designs[parity], p, pl.multiple_of(half * CHUNK, CHUNK), CHUNK)
         return 0
 
-    lax.fori_loop(0, chunks, chunk_body, 0)
+    total[...] = jnp.zeros_like(total)
+    lax.fori_loop(0, halves, two_chunks, 0)
 
 
 def pack_normals(total, packed):
@@ -304,24 +310,56 @@
         work[p] = jnp.where(column_ids == VALUE_ROW, right, matrix)
 
 
+def invert_rows(rows, lane, pairs):
+    names = lax.broadcasted_iota(jnp.int32, (8, 128), 0)
+    spread = [jnp.broadcast_to(rows[:, lane + j : lane + j + 1], (8, 128)) for j in range(8)]
+    tiles = [rows[:, i : i + 128] for i in range(0, rows.shape[1], 128)]
+    for pair in range(pairs):
+        top = 2 * pair
+        first, second = spread[top], spread[top + 1]
+        a, c = first[top : top + 1, :], first[top + 1 : top + 2, :]
+        b, d = second[top : top + 1, :], second[top + 1 : top + 2, :]
+        inverse = 1.0 / (a * d - b * c)
+        a, b, c, d = a * inverse, b * inverse, c * inverse, d * inverse
+
+        def step(x):
+            upper, lower = x[top : top + 1, :], x[top + 1 : top + 2, :]
+            new_upper = d * upper - b * lower
+            new_lower = a * lower - c * upper
+            x = x - first * new_upper - second * new_lower
+            return jnp.where(names == top, new_upper, jnp.where(names == top + 1, new_lower, x))
+
+        for j in range(top + 2, 2 * pairs):
+            spread[j] = step(spread[j])
+        tiles = [step(tile) for tile in tiles]
+    return jnp.concatenate(tiles, axis=1) if len(tiles) > 1 else tiles[0]
+
+
 def eliminate(work):
     for panel in range(WIDE // PANEL):
         top = panel * PANEL
         left = top // 128 * 128
-        blocks = [work[p, top : top + PANEL, left:WIDE] for p in range(2)]
-        panel_rows = lax.broadcasted_iota(jnp.int32, (PANEL, WIDE - left), 0)
-        for k in range(min(PANEL, VALUE_ROW - top)):
-            lane = top - left + k
+        groups = [
+            [work[p, top + i : top + i + 8, left:WIDE] for i in range(0, PANEL, 8)]
+            for p in range(2)
+        ]
+        for m in range(PANEL // 8):
+            lane = top - left + 8 * m
+            pairs = min(4, (BLOCK - top - 8 * m) // 2)
             for p in range(2):
-                block = blocks[p]
-                row = block[k : k + 1, :]
-                inverse = 1.0 / block[k : k + 1, lane : lane + 1]
-                scaled = row * inverse
-                updated = block - block[:, lane : lane + 1] * scaled
-                blocks[p] = jnp.where(panel_rows == k, scaled, updated)
+                solved = invert_rows(groups[p][m], lane, pairs)
+                for i in range(PANEL // 8):
+                    if i == m:
+                        continue
+                    rows = groups[p][i]
+                    taken = rows[:, lane : lane + 1] * solved[0:1, :]
+                    for j in range(1, 2 * pairs):
+                        taken = taken + rows[:, lane + j : lane + j + 1] * solved[j : j + 1, :]
+                    groups[p][i] = rows - taken
+                groups[p][m] = solved
         for p in range(2):
             inner = top % 128
-            weights = blocks[p]
+            weights = jnp.concatenate(groups[p], axis=0)
             pieces = []
             if inner > 0:
                 pieces.append(jnp.zeros((inner, WIDE - left), jnp.float32))
@@ -332,7 +370,7 @@
             factor = work[p, :, left : left + 128]
             if panel == WIDE // PANEL - 1:
                 lanes = lax.broadcasted_iota(jnp.int32, (WIDE, 128), 1)
-                factor = jnp.where(lanes == VALUE_ROW - left, 0.0, factor)
+                factor = jnp.where(lanes >= BLOCK - left, 0.0, factor)
             work[p, :, left:WIDE] = work[p, :, left:WIDE] - jnp.dot(
                 factor, tall, precision=HIGHEST, preferred_element_type=jnp.float32
             )
@@ -370,7 +408,7 @@
     arc_devices,
     order_devices,
     rows_here,
-    coef_ref,
+    coef_hbm,
     colat_hbm,
     lon_hbm,
     value_hbm,
@@ -379,12 +417,14 @@
     solution_ref,
     bias_ref,
     residual_ref,
+    coef_ref,
     colat,
     lon,
     value,
     arcs,
     kept,
-    design,
+    design0,
+    design1,
     window0,
     window1,
     starting,
@@ -410,7 +450,13 @@
     first_pair = ord_me * 2
     loads = []
     for i, (far, near) in enumerate(
-        [(colat_hbm, colat), (lon_hbm, lon), (value_hbm, value), (arc_hbm, arcs)]
+        [
+            (coef_hbm.at[ord_me], coef_ref),
+            (colat_hbm, colat),
+            (lon_hbm, lon),
+            (value_hbm, value),
+            (arc_hbm, arcs),
+        ]
     ):
         load = pltpu.make_async_copy(far, near, loaded.at[i])
         load.start()
@@ -435,14 +481,14 @@
 
     make_normals(
         first_pair,
-        rows_here // CHUNK,
+        rows_here // CHUNK // 2,
         coef_ref,
         colat,
         lon,
         value,
         arcs,
         kept,
-        design,
+        (design0, design1),
         (window0, window1, starting, total),
     )
     pack_normals(total, packed)
@@ -468,9 +514,8 @@
         peer = lax.rem(ord_me + k, order_devices)
         return remote("ord", peer, share.at[peer], arrived.at[source], send3.at[k], recv3.at[k])
 
-    def fit(k):
-        rank = lax.rem(ord_me + k, order_devices)
-        lane = pl.multiple_of(rank * span, span)
+    def fit(design, rank, lane):
+        lane = pl.multiple_of(lane, span)
         fitted = jnp.zeros((16, span), jnp.float32)
         for p in range(2):
             fitted = fitted + jnp.dot(
@@ -483,12 +528,20 @@
             share[rank, line : line + 1, :] = fitted[:, line * 128 : line * 128 + 128]
         share[rank, LINES : LINES + 1, :] = offset_row
 
-    def fit_and_send(k):
-        fit(k)
-        send_fit(k, ord_me).start()
-
-    each(1, order_devices, fit_and_send)
-    fit(0)
+    per_chunk = CHUNK // span
+    per_half = order_devices // 2
+    for parity, design in enumerate((design0, design1)):
+
+        def fit_and_send(k, design=design, parity=parity):
+            place = lax.rem(ord_me + 1 + k, per_half)
+            rank = (place // per_chunk * 2 + parity) * per_chunk + lax.rem(place, per_chunk)
+            fit(design, rank, place * span)
+
+            @pl.when(rank != ord_me)
+            def _():
+                send_fit(lax.rem(rank - ord_me + order_devices, order_devices), ord_me).start()
+
+        each(0, per_half, fit_and_send)
 
     arrived[ord_me] = share[ord_me]
     each(
@@ -523,7 +576,6 @@
     order_devices = lax.axis_size("ord")
     lines = (rows_here // 128, 128)
     table = jnp.asarray(recursion_table(2 * order_devices))
-    coef = lax.dynamic_index_in_dim(table, lax.axis_index("ord"), keepdims=False)
 
     def kernel(*refs):
         whole_kernel(arc_devices, order_devices, rows_here, *refs)
@@ -531,9 +583,7 @@
     vmem = pl.BlockSpec(memory_space=pltpu.VMEM)
     solved, bias, residual = pl.pallas_call(
         kernel,
-        in_specs=[pl.BlockSpec(memory_space=pltpu.SMEM)]
-        + [pl.BlockSpec(memory_space=pl.ANY)] * 4
-        + [vmem],
+        in_specs=[pl.BlockSpec(memory_space=pl.ANY)] * 5 + [vmem],
         out_specs=[vmem] * 3,
         out_shape=[
             jax.ShapeDtypeStruct((2, BLOCK), jnp.float32),
@@ -541,12 +591,14 @@
             jax.ShapeDtypeStruct((LINES, 128), jnp.float32),
         ],
         scratch_shapes=[
+            pltpu.SMEM((8, WIDE), jnp.float32),
             pltpu.VMEM(lines, jnp.float32),
             pltpu.VMEM(lines, jnp.float32),
             pltpu.VMEM(lines, jnp.bfloat16),
             pltpu.VMEM(lines, jnp.int32),
             pltpu.VMEM(lines, jnp.float32),
-            pltpu.VMEM((2, ROWS, rows_here), jnp.bfloat16),
+            pltpu.VMEM((2, ROWS, rows_here // 2), jnp.bfloat16),
+            pltpu.VMEM((2, ROWS, rows_here // 2), jnp.bfloat16),
             pltpu.VMEM((2 * TILES * STRIDE, 128), jnp.float32),
             pltpu.VMEM((2 * TILES * STRIDE, 128), jnp.float32),
             pltpu.VMEM((4 * TILES, 128), jnp.float32),
@@ -557,7 +609,7 @@
             pltpu.VMEM((2, WIDE, WIDE), jnp.float32),
             pltpu.VMEM((order_devices, 16, 128), jnp.float32),
             pltpu.VMEM((order_devices, 16, 128), jnp.float32),
-            pltpu.SemaphoreType.DMA((4,)),
+            pltpu.SemaphoreType.DMA((5,)),
         ]
         + [pltpu.SemaphoreType.DMA((arc_devices,))] * 4
         + [pltpu.SemaphoreType.DMA((order_devices,))] * 2,
@@ -566,7 +618,7 @@
         ),
         name="whole",
     )(
-        coef,
+        table,
         obs_colat.reshape(lines),
         obs_lon.reshape(lines),
         obs_value.reshape(lines),

time: 81.5 us -> 64.8 us (0.80)
  Pallas kernels: 76.8 us -> 61.7 us
  local copies, waits for them, and re-layouts: 3.74 us -> 2.35 us
    pallas_call x1, Pallas kernels: 76.8 us -> 61.7 us  [per_device(): pl.pallas_call(kernel, in_specs=[pl.BlockSpec(memory_space=pl.ANY)] * 5 +...]
    dynamic_slice x1 -> x0, local copies, waits for them, and re-layouts: 1.39 us -> none  [per_device(): lax.dynamic_index_in_dim(table, lax.axis_index('ord'), keepdims=False)]
where the time goes in v3:
time: 64.8 us; the launch traced here: 64.7 us
  Pallas kernels  61.7 us (95%)
  local copies, waits for them, and re-layouts  2.35 us (4%)
  between operations  0.66 us (1%)
    pallas_call x1, Pallas kernels, per_device(): pl.pallas_call(kernel, in_specs=[pl.BlockSpec(memory_space=pl.ANY)] * 5 +...  61.7 us
    unnamed x7, local copies, waits for them, and re-layouts  2.35 us

profile of v3, /device:TPU:1, one launch (start us, length us, event | category | flops | bytes accessed | tf_op | source)
XLA Modules:
  0.0 64.7 jit_solution(4183187795615878919)
XLA Ops:
  0.6 61.7 %whole.1 = (f32[2,252]{1,0:T(2,128)}, f32[1,16]{1,0:T(1,128)}, f32[12,128]{1,0:T(8,128)}) custom-call(f32[16,8,256]{2,1,0:T(8,128)} %constant.2.clone.refs_0_, f32[192,128]{1,0:T(8,128)} %bitcast.6, f32[192,128]{1,0:T(8,128)} %bitcast.7, bf16[192,128]{1,0:T(8,128)(2,1)} %bitcast.9, s32[192,128]{1,0:T(8,128)} %bitcast.8, f32[2,252]{1,0:T(2,128)} %refs_5_.1), custom_call_target="tpu_custom_call" | custom-call | tf_op jit(solution)/shard_map/whole/pallas_call | solution.py:584
  62.3 0.0 copy-start
  62.3 0.0 copy-start.1
  62.3 1.2 %copy.12 = f32[2,252]{1,0:T(2,128)} copy(f32[2,252]{1,0:T(2,128)} %get-tuple-element.12) | data formatting | bytes 4032
  63.6 0.0 copy-done.1
  63.6 0.5 copy.13
  64.1 0.0 copy-done
  64.1 0.6 copy.14
Async XLA Ops:
  62.3 1.8 %copy-start = (f32[12,128]{1,0:T(8,128)S(1)}, f32[12,128]{1,0:T(8,128)}, u32[]{:S(2)}) copy-start(f32[12,128]{1,0:T(8,128)} %get-tuple-element.8) | copy-start | bytes 18436
  62.3 1.2 %copy-start.1 = (f32[1,16]{1,0:T(1,128)S(1)}, f32[1,16]{1,0:T(1,128)}, u32[]{:S(2)}) copy-start(f32[1,16]{1,0:T(1,128)} %get-tuple-element.7) | copy-start | bytes 196

commit v4 on v3

--- a/solution.py
+++ b/solution.py
@@ -515,15 +515,14 @@
         return remote("ord", peer, share.at[peer], arrived.at[source], send3.at[k], recv3.at[k])
 
     def fit(design, rank, lane):
-        lane = pl.multiple_of(lane, span)
         fitted = jnp.zeros((16, span), jnp.float32)
         for p in range(2):
             fitted = fitted + jnp.dot(
                 split[p],
-                design[p, 0:WIDE, pl.ds(lane, span)],
+                design[p, 0:WIDE, lane : lane + span],
                 preferred_element_type=jnp.float32,
             )
-        fitted = jnp.sum(fitted, axis=0, keepdims=True)
+        fitted = jnp.sum(fitted[0:8], axis=0, keepdims=True)
         for line in range(LINES):
             share[rank, line : line + 1, :] = fitted[:, line * 128 : line * 128 + 128]
         share[rank, LINES : LINES + 1, :] = offset_row
@@ -532,16 +531,20 @@
     per_half = order_devices // 2
     for parity, design in enumerate((design0, design1)):
 
-        def fit_and_send(k, design=design, parity=parity):
-            place = lax.rem(ord_me + 1 + k, per_half)
-            rank = (place // per_chunk * 2 + parity) * per_chunk + lax.rem(place, per_chunk)
-            fit(design, rank, place * span)
+        def rank_of(place, parity=parity):
+            return (place // per_chunk * 2 + parity) * per_chunk + lax.rem(place, per_chunk)
+
+        for place in range(per_half):
+            fit(design, (place // per_chunk * 2 + parity) * per_chunk + place % per_chunk, place * span)
+
+        def send(k):
+            rank = rank_of(lax.rem(ord_me + 1 + k, per_half))
 
             @pl.when(rank != ord_me)
             def _():
                 send_fit(lax.rem(rank - ord_me + order_devices, order_devices), ord_me).start()
 
-        each(0, per_half, fit_and_send)
+        each(0, per_half, send)
 
     arrived[ord_me] = share[ord_me]
     each(
@@ -568,6 +571,15 @@
     )
     end_reduce()
     each(1, order_devices, lambda k: send_fit(k, ord_me).wait_send())
+
+
+def hand_on(*refs):
+    sems = refs[6]
+    copies = [pltpu.make_async_copy(refs[i], refs[3 + i], sems.at[i]) for i in range(3)]
+    for copy in copies:
+        copy.start()
+    for copy in copies:
+        copy.wait()
 
 
 def per_device(obs_colat, obs_lon, obs_value, obs_arc, reg_weight):
@@ -625,6 +637,15 @@
         obs_arc.reshape(lines),
         reg_weight,
     )
+    shapes = [jax.ShapeDtypeStruct(x.shape, x.dtype) for x in (solved, bias, residual)]
+    solved, bias, residual = pl.pallas_call(
+        hand_on,
+        in_specs=[pl.BlockSpec(memory_space=pl.ANY)] * 3,
+        out_specs=[pl.BlockSpec(memory_space=pl.ANY)] * 3,
+        out_shape=shapes,
+        scratch_shapes=[pltpu.SemaphoreType.DMA((3,))],
+        name="hand_on",
+    )(solved, bias, residual)
     return (solved, bias.reshape(-1), residual.reshape(-1))
 
 

time: 64.8 us -> 64.4 us (level)
  local copies, waits for them, and re-layouts: 2.35 us -> 0 us
  Pallas kernels: 61.7 us -> 63.5 us
    unnamed x7 -> x0, local copies, waits for them, and re-layouts: 2.35 us -> none
    pallas_call x0 -> x1, Pallas kernels: none -> 1.39 us  [per_device(): pl.pallas_call(hand_on, in_specs=[pl.BlockSpec(memory_space=pl.ANY)] * 3,...]
where the time goes in v4:
time: 64.4 us; the launch traced here: 64.3 us
  Pallas kernels  63.5 us (99%)
  between operations  0.8 us (1%)
    pallas_call x1, Pallas kernels, per_device(): pl.pallas_call(kernel, in_specs=[pl.BlockSpec(memory_space=pl.ANY)] * 5 +...  62.1 us
    pallas_call x1, Pallas kernels, per_device(): pl.pallas_call(hand_on, in_specs=[pl.BlockSpec(memory_space=pl.ANY)] * 3,...  1.39 us

profile of v4, /device:TPU:1, one launch (start us, length us, event | category | flops | bytes accessed | tf_op | source)
XLA Modules:
  0.0 64.3 jit_solution(6408241412262713015)
XLA Ops:
  0.6 62.1 %whole.1 = (f32[2,252]{1,0:T(2,128)}, f32[1,16]{1,0:T(1,128)}, f32[12,128]{1,0:T(8,128)}) custom-call(f32[16,8,256]{2,1,0:T(8,128)} %constant.2.clone.refs_0_, f32[192,128]{1,0:T(8,128)} %bitcast.6, f32[192,128]{1,0:T(8,128)} %bitcast.7, bf16[192,128]{1,0:T(8,128)(2,1)} %bitcast.9, s32[192,128]{1,0:T(8,128)} %bitcast.8, f32[2,252]{1,0:T(2,128)} %refs_5_.1), custom_call_target="tpu_custom_call" | custom-call | tf_op jit(solution)/shard_map/whole/pallas_call | solution.py:596
  62.7 1.4 %hand_on.1 = (f32[2,252]{1,0:T(2,128)}, f32[1,16]{1,0:T(1,128)}, f32[12,128]{1,0:T(8,128)}) custom-call(f32[2,252]{1,0:T(2,128)} %get-tuple-element.9.refs_0_, f32[1,16]{1,0:T(1,128)} %get-tuple-element.10.refs_1_, f32[12,128]{1,0:T(8,128)} %get-tuple-element.11.refs_2_), custom_call_target="tpu_custom_call" | custom-call | tf_op jit(solution)/shard_map/hand_on/pallas_call | solution.py:641

commit v5 on v4

--- a/solution.py
+++ b/solution.py
@@ -15,7 +15,7 @@
 ROWS = WIDE + ARC_DEV
 VALUE_ROW = 255
 COUNT_ROW = 254
-STRIDE = 20
+STRIDE = 17
 HALF_PI = float(np.float32(0.5 * math.pi))
 HALF_PI_REST = 0.5 * math.pi - HALF_PI
 COSINE = [(-1.0) ** k * (2.0 * math.pi) ** (2 * k) / math.factorial(2 * k) for k in range(11)]
@@ -107,12 +107,9 @@
         )
 
     def chunk_body(half, parity):
-        design, other = designs[parity], designs[1 - parity]
+        design = designs[parity]
         line = pl.multiple_of((2 * half + parity) * TILES, TILES)
         first_lane = pl.multiple_of(half * CHUNK, CHUNK)
-        other_lane = first_lane
-        if parity == 0:
-            other_lane = lax.rem(half + halves - 1, halves) * CHUNK
         t = []
         for v in range(GROUPS):
             rows = pl.ds(pl.multiple_of(line + v * 8, 8), 8)
@@ -136,19 +133,20 @@
                 return kept[rows, :]
             return jnp.where(arcs[rows, :] < ARC_DEV, 1.0, 0.0)
 
-        def convert(window, row):
+        def convert(window, row, first=0, last=2 * TILES):
             row = pl.multiple_of(row, 16)
-            for p in range(2):
-                for tile in range(TILES):
-                    source = (p * TILES + tile) * STRIDE
-                    lane = pl.multiple_of(first_lane + tile * 128, 128)
-                    design[p, pl.ds(row, 16), pl.ds(lane, 128)] = window[
-                        source : source + 16, :
-                    ].astype(jnp.bfloat16)
-
-        def columns16(window, base, carried, turning, last):
+            for unit in range(first, last):
+                p, tile = unit // TILES, unit % TILES
+                lane = pl.multiple_of(first_lane + tile * 128, 128)
+                design[p, pl.ds(row, 16), pl.ds(lane, 128)] = window[
+                    unit * STRIDE : unit * STRIDE + 16, :
+                ].astype(jnp.bfloat16)
+
+        def columns16(window, base, carried, turning, last, done, row):
             previous, before = carried
+            units = 2 * TILES // 16
             for inner in range(16):
+                convert(done, row, inner * units, inner * units + units)
                 column = base + inner
                 rising = [coef_ref[2 * p, column] for p in range(2)]
                 falling = [coef_ref[2 * p + 1, column] for p in range(2)]
@@ -169,12 +167,9 @@
 
         def columns32(block, carried, turning):
             base = block * 32
-            quarter = CHUNK // 4
-            lane = pl.multiple_of(other_lane + lax.rem(block, 4) * quarter, quarter)
-            convert(window1, lax.rem(base + (WIDE - 16), WIDE))
-            carried = columns16(window0, base, carried, turning, False)
-            convert(window0, base)
-            return columns16(window1, base + 16, carried, turning, True)
+            row = lax.rem(base + (WIDE - 16), WIDE)
+            carried = columns16(window0, base, carried, turning, False, window1, row)
+            return columns16(window1, base + 16, carried, turning, True, window0, base)
 
         zeros = tuple(jnp.zeros((8, 128), jnp.float32) for _ in chains)
         carried = (zeros, tuple(seed(p, v) for p, v in chains))

time: 64.4 us -> 63.3 us (0.983)
  Pallas kernels: 63.5 us -> 62.3 us
    pallas_call x1, Pallas kernels: 62.1 us -> 60.9 us  [per_device(): pl.pallas_call(kernel, in_specs=[pl.BlockSpec(memory_space=pl.ANY)] * 5 +...]
where the time goes in v5:
time: 63.3 us; the launch traced here: 63.1 us
  Pallas kernels  62.3 us (98%)
  between operations  0.8 us (1%)
    pallas_call x1, Pallas kernels, per_device(): pl.pallas_call(kernel, in_specs=[pl.BlockSpec(memory_space=pl.ANY)] * 5 +...  60.9 us
    pallas_call x1, Pallas kernels, per_device(): pl.pallas_call(hand_on, in_specs=[pl.BlockSpec(memory_space=pl.ANY)] * 3,...  1.39 us

profile of v5, /device:TPU:1, one launch (start us, length us, event | category | flops | bytes accessed | tf_op | source)
XLA Modules:
  0.0 63.1 jit_solution(12445999233748717731)
XLA Ops:
  0.6 60.9 %whole.1 = (f32[2,252]{1,0:T(2,128)}, f32[1,16]{1,0:T(1,128)}, f32[12,128]{1,0:T(8,128)}) custom-call(f32[16,8,256]{2,1,0:T(8,128)} %constant.2.clone.refs_0_, f32[192,128]{1,0:T(8,128)} %bitcast.6, f32[192,128]{1,0:T(8,128)} %bitcast.7, bf16[192,128]{1,0:T(8,128)(2,1)} %bitcast.9, s32[192,128]{1,0:T(8,128)} %bitcast.8, f32[2,252]{1,0:T(2,128)} %refs_5_.1), custom_call_target="tpu_custom_call" | custom-call | tf_op jit(solution)/shard_map/whole/pallas_call | solution.py:591
  61.5 1.4 %hand_on.1 = (f32[2,252]{1,0:T(2,128)}, f32[1,16]{1,0:T(1,128)}, f32[12,128]{1,0:T(8,128)}) custom-call(f32[2,252]{1,0:T(2,128)} %get-tuple-element.9.refs_0_, f32[1,16]{1,0:T(1,128)} %get-tuple-element.10.refs_1_, f32[12,128]{1,0:T(8,128)} %get-tuple-element.11.refs_2_), custom_call_target="tpu_custom_call" | custom-call | tf_op jit(solution)/shard_map/hand_on/pallas_call | solution.py:636

commit v6 on v5

--- a/solution.py
+++ b/solution.py
@@ -529,17 +529,21 @@
         def rank_of(place, parity=parity):
             return (place // per_chunk * 2 + parity) * per_chunk + lax.rem(place, per_chunk)
 
-        for place in range(per_half):
-            fit(design, (place // per_chunk * 2 + parity) * per_chunk + place % per_chunk, place * span)
-
-        def send(k):
-            rank = rank_of(lax.rem(ord_me + 1 + k, per_half))
-
-            @pl.when(rank != ord_me)
-            def _():
-                send_fit(lax.rem(rank - ord_me + order_devices, order_devices), ord_me).start()
-
-        each(0, per_half, send)
+        for first in range(0, per_half, per_chunk):
+            for place in range(first, first + per_chunk):
+                owner = (first // per_chunk * 2 + parity) * per_chunk + place - first
+                fit(design, owner, place * span)
+
+            def send(k, first=first, rank_of=rank_of):
+                rank = rank_of(first + lax.rem(ord_me + 1 + k, per_chunk))
+
+                @pl.when(rank != ord_me)
+                def _():
+                    send_fit(
+                        lax.rem(rank - ord_me + order_devices, order_devices), ord_me
+                    ).start()
+
+            each(0, per_chunk, send)
 
     arrived[ord_me] = share[ord_me]
     each(

time: 63.3 us -> 62 us (0.979)
  Pallas kernels: 62.3 us -> 61 us
    pallas_call x1, Pallas kernels: 60.9 us -> 59.6 us  [per_device(): pl.pallas_call(kernel, in_specs=[pl.BlockSpec(memory_space=pl.ANY)] * 5 +...]
where the time goes in v6:
time: 62 us; the launch traced here: 61.8 us
  Pallas kernels  61 us (98%)
  between operations  0.8 us (1%)
    pallas_call x1, Pallas kernels, per_device(): pl.pallas_call(kernel, in_specs=[pl.BlockSpec(memory_space=pl.ANY)] * 5 +...  59.6 us
    pallas_call x1, Pallas kernels, per_device(): pl.pallas_call(hand_on, in_specs=[pl.BlockSpec(memory_space=pl.ANY)] * 3,...  1.39 us

profile of v6, /device:TPU:1, one launch (start us, length us, event | category | flops | bytes accessed | tf_op | source)
XLA Modules:
  0.0 61.8 jit_solution(16685598900977597203)
XLA Ops:
  0.6 59.6 %whole.1 = (f32[2,252]{1,0:T(2,128)}, f32[1,16]{1,0:T(1,128)}, f32[12,128]{1,0:T(8,128)}) custom-call(f32[16,8,256]{2,1,0:T(8,128)} %constant.2.clone.refs_0_, f32[192,128]{1,0:T(8,128)} %bitcast.6, f32[192,128]{1,0:T(8,128)} %bitcast.7, bf16[192,128]{1,0:T(8,128)(2,1)} %bitcast.9, s32[192,128]{1,0:T(8,128)} %bitcast.8, f32[2,252]{1,0:T(2,128)} %refs_5_.1), custom_call_target="tpu_custom_call" | custom-call | tf_op jit(solution)/shard_map/whole/pallas_call | solution.py:595
  60.3 1.4 %hand_on.1 = (f32[2,252]{1,0:T(2,128)}, f32[1,16]{1,0:T(1,128)}, f32[12,128]{1,0:T(8,128)}) custom-call(f32[2,252]{1,0:T(2,128)} %get-tuple-element.9.refs_0_, f32[1,16]{1,0:T(1,128)} %get-tuple-element.10.refs_1_, f32[12,128]{1,0:T(8,128)} %get-tuple-element.11.refs_2_), custom_call_target="tpu_custom_call" | custom-call | tf_op jit(solution)/shard_map/hand_on/pallas_call | solution.py:640
